TPU v7x, 128 devices: a whole 4x4x4 slice. The times are simulated.
128 devices in a mesh: ctx: 32 (over z, y, x_lo), tp: 4 (over x_hi, core).
Axes of the slice: x: 4 (x_hi: 2, x_lo: 2; x = x_hi * 2 + x_lo), y: 4, z: 4, core: 2. Of those that a mesh axis runs over, the one named last changes fastest.
Arguments:
- query_gate: bfloat16 [2048, 16384], P('tp', 'ctx'), may hold values from -6 to 6
- key_branch: bfloat16 [2048, 16384], P('tp', 'ctx'), may hold values from -6 to 6
- value_branch: bfloat16 [2048, 16384], P('tp', 'ctx'), may hold values from -6 to 6
- filter_taps: float32 [2048, 16384], P(('tp', 'ctx')), may hold values from -2 to 2
- skip_gain: float32 [2048], P(('tp', 'ctx')), may hold values from -4 to 4
- out_weight: bfloat16 [2048, 4096], P('tp'), may hold values from -0.09375 to 0.09375
- out_grad: bfloat16 [16384, 4096], P('ctx', 'tp'), may hold values from -6 to 6
Outputs:
- grad_query: bfloat16 [2048, 16384], P('tp', 'ctx')
- grad_key: bfloat16 [2048, 16384], P('tp', 'ctx')
- grad_value: bfloat16 [2048, 16384], P('tp', 'ctx')
- grad_filter: float32 [2048, 16384], P(('tp', 'ctx'))
- grad_skip: float32 [2048], P(('tp', 'ctx'))
- grad_weight: float32 [2048, 4096], P('tp', 'ctx')
All inputs are finite; a program needn't handle non-finite values.
Results may differ from a plain program's by a relative error of at most 0.0058.
Values may be sent and summed in bfloat16 or wider, within the bound.
A program may use at most 128 MiB of HBM per device.

v0:
```python
import numpy as np
import ml_dtypes
import jax
import jax.numpy as jnp
from jax import lax
from jax.experimental import pallas as pl
from jax.experimental.pallas import tpu as pltpu
from jax.sharding import PartitionSpec as P

ROWS = 64
COLS = 256
LANES = 128
CHANS = 16
SEQ_BLOCKS = 32


def bf16_pair(values):
    high = values.astype(ml_dtypes.bfloat16)
    low = (values - high.astype(np.float64)).astype(ml_dtypes.bfloat16)
    return high, low


def tables():
    ka = np.arange(ROWS) + 0.5
    phase_a = 2.0 * np.pi * np.outer(ka, np.arange(ROWS)) / (2 * ROWS)
    first = np.concatenate([np.cos(phase_a), -np.sin(phase_a)], axis=0)
    high, low = bf16_pair(first)
    first = np.concatenate([high, low, high], axis=1)
    last = np.concatenate([np.cos(phase_a).T, np.sin(phase_a).T], axis=1) / (ROWS * COLS)
    last = last.astype(ml_dtypes.bfloat16)
    last = np.concatenate([last, last], axis=1)
    phase_t = 2.0 * np.pi * np.outer(ka, np.arange(COLS)) / (2 * ROWS * COLS)
    turn = np.concatenate([np.cos(phase_t), np.sin(phase_t)], axis=1).astype(np.float32)
    phase_b = 2.0 * np.pi * (np.outer(np.arange(COLS), np.arange(COLS)) % COLS) / COLS
    cos_b, sin_b = np.cos(phase_b), np.sin(phase_b)
    second = np.block([[cos_b, -sin_b], [sin_b, cos_b]]).astype(ml_dtypes.bfloat16)
    return first, last, turn, second


def dot(left, right):
    return jnp.dot(left, right, preferred_element_type=jnp.float32)


def turned(re, im, turn_ref):
    cos, sin = turn_ref[:, :COLS], turn_ref[:, COLS:]
    return re * cos + im * sin, im * cos - re * sin


def take_blocks(blocks_ref, grid):
    def step(s, carry):
        block = blocks_ref[s].astype(jnp.float32)
        for part in range(4):
            rows = pl.ds(pl.multiple_of(s * 32 + part // 2 * CHANS, CHANS), CHANS)
            grid[part % 2, rows, :] = block[:, part * LANES : (part + 1) * LANES]
        return carry

    lax.fori_loop(0, SEQ_BLOCKS, step, 0, unroll=4)


def second_stage(mixed, second_ref, out):
    def step(i, carry):
        rows = pl.ds(pl.multiple_of(i * 256, 256), 256)
        out[rows, :] = dot(mixed[rows, :], second_ref[...])
        return carry

    lax.fori_loop(0, CHANS * ROWS // 256, step, 0)


def spectrum_of(grid, first_ref, turn_ref, second_ref, mixed, out, wide):
    def step(c, carry):
        rows = pl.ds(c, ROWS, stride=CHANS)
        signal = jnp.concatenate([grid[0, rows, :], grid[1, rows, :]], axis=1)
        high = signal.astype(jnp.bfloat16)
        if wide:
            low = (signal - high.astype(jnp.float32)).astype(jnp.bfloat16)
            left, right = first_ref[...], jnp.concatenate([high, high, low], axis=0)
        else:
            left, right = first_ref[:, : 2 * ROWS], jnp.concatenate([high, high], axis=0)
        part = dot(left, right)
        re, im = turned(part[:ROWS], part[ROWS:], turn_ref)
        rows = pl.ds(pl.multiple_of(c * ROWS, ROWS), ROWS)
        mixed[rows, :COLS] = re.astype(jnp.bfloat16)
        mixed[rows, COLS:] = im.astype(jnp.bfloat16)
        return carry

    lax.fori_loop(0, CHANS, step, 0, unroll=4)
    second_stage(mixed, second_ref, out)


def product_to(mixed, left, right, conj):
    def step(i, carry):
        rows = pl.ds(pl.multiple_of(i * ROWS, ROWS), ROWS)
        lr, li = left[rows, :COLS], left[rows, COLS:]
        rr, ri = right[rows, :COLS], right[rows, COLS:]
        if conj:
            re, im = lr * rr + li * ri, li * rr - lr * ri
        else:
            re, im = lr * rr - li * ri, -(lr * ri + li * rr)
        mixed[rows, :COLS] = re.astype(jnp.bfloat16)
        mixed[rows, COLS:] = im.astype(jnp.bfloat16)
        return carry

    lax.fori_loop(0, CHANS, step, 0, unroll=2)


def signal_of(mixed, last_ref, turn_ref, second_ref, spec, grid):
    second_stage(mixed, second_ref, spec)

    def step(c, carry):
        rows = pl.ds(pl.multiple_of(c * ROWS, ROWS), ROWS)
        re, im = turned(spec[rows, :COLS], spec[rows, COLS:], turn_ref)
        both = jnp.concatenate([re, im], axis=0)
        high = both.astype(jnp.bfloat16)
        low = (both - high.astype(jnp.float32)).astype(jnp.bfloat16)
        signal = dot(last_ref[...], jnp.concatenate([high, low], axis=0))
        for half in range(2):
            grid[half, pl.ds(c, ROWS, stride=CHANS), :] = signal[:, half * LANES : (half + 1) * LANES]
        return carry

    lax.fori_loop(0, CHANS, step, 0, unroll=4)


def give_blocks(grid, blocks_ref):
    def step(s, carry):
        for part in range(4):
            rows = pl.ds(pl.multiple_of(s * 32 + part // 2 * CHANS, CHANS), CHANS)
            blocks_ref[s, :, part * LANES : (part + 1) * LANES] = grid[part % 2, rows, :].astype(jnp.bfloat16)
        return carry

    lax.fori_loop(0, SEQ_BLOCKS, step, 0, unroll=4)


def conv_kernel(
    gated_ref, taps_ref, skip_ref, first_ref, last_ref, turn_ref, second_ref,
    conv_ref, taps_spec, gated_spec, grid, mixed, spec,
):
    for a in range(ROWS):
        for half in range(2):
            start = a * COLS + half * LANES
            grid[half, a * CHANS : (a + 1) * CHANS, :] = taps_ref[:, start : start + LANES]
    lane = lax.broadcasted_iota(jnp.int32, (CHANS, LANES), 1)
    grid[0, :CHANS, :] += jnp.where(lane == 0, skip_ref[...], 0.0)
    spectrum_of(grid, first_ref, turn_ref, second_ref, mixed, taps_spec, True)
    take_blocks(gated_ref, grid)
    spectrum_of(grid, first_ref, turn_ref, second_ref, mixed, gated_spec, False)
    product_to(mixed, taps_spec, gated_spec, False)
    signal_of(mixed, last_ref, turn_ref, second_ref, spec, grid)
    give_blocks(grid, conv_ref)


def grad_kernel(
    grad_ref, gated_ref, taps_spec, gated_spec, first_ref, last_ref, turn_ref, second_ref,
    back_ref, taps_grad_ref, skip_grad_ref, grid, mixed, spec, grad_spec,
):
    take_blocks(grad_ref, grid)
    spectrum_of(grid, first_ref, turn_ref, second_ref, mixed, grad_spec, False)
    product_to(mixed, taps_spec, grad_spec, True)
    signal_of(mixed, last_ref, turn_ref, second_ref, spec, grid)
    give_blocks(grid, back_ref)
    product_to(mixed, gated_spec, grad_spec, True)
    signal_of(mixed, last_ref, turn_ref, second_ref, spec, grid)
    for a in range(ROWS):
        for half in range(2):
            start = a * COLS + half * LANES
            taps_grad_ref[:, start : start + LANES] = grid[half, a * CHANS : (a + 1) * CHANS, :]

    def step(s, total):
        return total + grad_ref[s].astype(jnp.float32) * gated_ref[s].astype(jnp.float32)

    total = lax.fori_loop(0, SEQ_BLOCKS, step, jnp.zeros((CHANS, 2 * COLS), jnp.float32))
    skip_grad_ref[...] = jnp.sum(total, axis=1, keepdims=True)


def vmem_specs(count):
    return [pl.BlockSpec(memory_space=pltpu.VMEM)] * count


def body(query_gate, key_branch, value_branch, filter_taps, skip_gain, out_weight, out_grad):
    first, last, turn, second = [jnp.asarray(t) for t in tables()]
    full_grad = lax.all_gather(out_grad, "tp", axis=1, tiled=True)
    query_f = query_gate.astype(jnp.float32)
    key_f = key_branch.astype(jnp.float32)
    value_f = value_branch.astype(jnp.float32)
    blocks = (SEQ_BLOCKS, CHANS, 2 * COLS)
    spec_shape = jax.ShapeDtypeStruct((CHANS * ROWS, 2 * COLS), jnp.float32)
    grid = pltpu.VMEM((2, CHANS * ROWS, LANES), jnp.float32)
    mixed_s = pltpu.VMEM((CHANS * ROWS, 2 * COLS), jnp.bfloat16)
    spec_s = pltpu.VMEM((CHANS * ROWS, 2 * COLS), jnp.float32)
    params = pltpu.CompilerParams(vmem_limit_bytes=40 * 1024 * 1024)

    gated = (key_f * value_f).astype(jnp.bfloat16)
    gated_chan = lax.all_to_all(gated.reshape(blocks), "ctx", split_axis=0, concat_axis=0)
    conv_chan, taps_spec, gated_spec = pl.pallas_call(
        conv_kernel,
        out_shape=(jax.ShapeDtypeStruct(blocks, jnp.bfloat16), spec_shape, spec_shape),
        in_specs=vmem_specs(7),
        out_specs=vmem_specs(3),
        scratch_shapes=[grid, mixed_s, spec_s],
        compiler_params=params,
    )(gated_chan, filter_taps, skip_gain[:, None], first, last, turn, second)
    conv_out = lax.all_to_all(conv_chan, "ctx", split_axis=0, concat_axis=0).reshape(query_gate.shape)
    conv_f = conv_out.astype(jnp.float32)
    grad_mixed = lax.dot_general(
        out_weight, full_grad, (((1,), (1,)), ((), ())), preferred_element_type=jnp.float32
    )
    grad_conv = (grad_mixed * query_f).astype(jnp.bfloat16)
    grad_chan = lax.all_to_all(grad_conv.reshape(blocks), "ctx", split_axis=0, concat_axis=0)
    mixed = (query_f * conv_f).astype(jnp.bfloat16)
    terms = lax.dot_general(mixed, full_grad, (((1,), (0,)), ((), ())), preferred_element_type=jnp.float32)
    terms = terms.astype(jnp.bfloat16).reshape(terms.shape[0], SEQ_BLOCKS, -1).transpose(1, 0, 2)
    terms = lax.all_to_all(terms, "ctx", split_axis=0, concat_axis=0)
    grad_weight = jnp.sum(terms.astype(jnp.float32), axis=0)
    back_chan, grad_filter, grad_skip = pl.pallas_call(
        grad_kernel,
        out_shape=(
            jax.ShapeDtypeStruct(blocks, jnp.bfloat16),
            jax.ShapeDtypeStruct(filter_taps.shape, jnp.float32),
            jax.ShapeDtypeStruct((CHANS, 1), jnp.float32),
        ),
        in_specs=vmem_specs(8),
        out_specs=vmem_specs(3),
        scratch_shapes=[grid, mixed_s, spec_s, spec_s],
        compiler_params=params,
    )(grad_chan, gated_chan, taps_spec, gated_spec, first, last, turn, second)
    grad_gated = lax.all_to_all(back_chan, "ctx", split_axis=0, concat_axis=0).reshape(query_gate.shape)
    grad_query = (grad_mixed * conv_f).astype(jnp.bfloat16)
    grad_gated_f = grad_gated.astype(jnp.float32)
    grad_key = (grad_gated_f * value_f).astype(jnp.bfloat16)
    grad_value = (grad_gated_f * key_f).astype(jnp.bfloat16)
    return (grad_query, grad_key, grad_value, grad_filter, grad_skip[:, 0], grad_weight)


def solution(mesh):
    placed = (
        P("tp", "ctx"),
        P("tp", "ctx"),
        P("tp", "ctx"),
        P(("tp", "ctx"), None),
        P(("tp", "ctx")),
        P("tp", None),
        P("ctx", "tp"),
    )
    return jax.shard_map(
        body,
        mesh=mesh,
        in_specs=placed,
        out_specs=(
            P("tp", "ctx"),
            P("tp", "ctx"),
            P("tp", "ctx"),
            P(("tp", "ctx"), None),
            P(("tp", "ctx")),
            P("tp", "ctx"),
        ),
        check_vma=False,
    )
```

profile of v0, /device:TPU:14, one launch (start us, length us, event | category | flops | bytes accessed | tf_op | source)
XLA Modules:
  0.0 173.6 jit_solution(2315946587583463897)
XLA Ops:
  7.2 0.0 all-gather.2.cloned.1.call-start
  7.2 0.7 all-gather.2.cloned.1.call-update
  7.9 2.1 %fusion.1 = bf16[512,512]{1,0:T(8,128)(2,1)} fusion(bf16[512,512]{1,0:T(8,128)(2,1)} %param.13, bf16[512,512]{1,0:T(8,128)(2,1)} %param.12), kind=kLoop, calls=%fused_computation.10 | loop fusion | flops 1048576 | bytes 1572864 | tf_op jit(solution)/shard_map/convert_element_type | solution.py:191
  10.0 9.4 %all-to-all-start = ((bf16[32,16,512]{2,1,0:T(8,128)(2,1)}), bf16[32,16,512]{2,1,0:T(8,128)(2,1)S(1)}, u32[]{:S(2)}, u32[]{:S(2)}) async-start(bf16[32,16,512]{2,1,0:T(8,128)(2,1)} %bitcast), calls=%async_computation | async-start | bytes 1048576 | tf_op jit(solution)/shard_map/all_to_all | solution.py:192
  19.5 0.7 copy.19.skip_ref
  20.2 11.3 %all-to-all-done.gated_ref = bf16[32,16,512]{2,1,0:T(8,128)(2,1)S(1)} async-done(((bf16[32,16,512]{2,1,0:T(8,128)(2,1)}), bf16[32,16,512]{2,1,0:T(8,128)(2,1)S(1)}, u32[]{:S(2)}, u32[]{:S(2)}) %all-to-all-start) | async-done | bytes 524320 | tf_op jit(solution)/shard_map/all_to_all | solution.py:192
  31.6 1.0 copy-done.2
  32.6 1.3 copy-done.4
  33.9 0.9 copy-done.5
  34.8 0.8 copy-done.8
  35.6 0.8 copy-done.10
  36.4 7.6 %shard_map.154 = (bf16[32,16,512]{2,1,0:T(8,128)(2,1)S(1)}, f32[1024,512]{1,0:T(8,128)S(1)}, f32[1024,512]{1,0:T(8,128)S(1)}) custom-call(bf16[32,16,512]{2,1,0:T(8,128)(2,1)S(1)} %all-to-all-done.gated_ref, f32[16,16384]{1,0:T(8,128)S(1)} %copy-done.4, f32[16,1]{1,0:T(8,128)S(1)} %copy.19.skip_ref, bf16[128,192]{1,0:T(8,128)(2,1)S(1)} %copy-done.8, ...), custom_call_target="tpu_custom_call" | custom-call | tf_op jit(solution)/shard_map/pallas_call | solution.py:193
  44.0 0.0 copy-start
  44.0 1.3 copy-done
  45.4 15.6 %all_to_all.25 = bf16[32,16,512]{2,1,0:T(8,128)(2,1)} all-to-all(bf16[32,16,512]{2,1,0:T(8,128)(2,1)S(1)} %get-tuple-element.12), channel_id=1, replica_groups=mesh['ctx'=32,'tp'=4] {'ctx'}, dimensions={0} | all-to-all | bytes 1048576 | tf_op jit(solution)/shard_map/all_to_all | solution.py:201
  61.0 0.0 all-gather.2.cloned.1.call-done
  61.0 0.0 copy-start.1
  61.0 7.0 %fusion.2 = (bf16[512,512]{1,0:T(8,128)(2,1)S(1)}, bf16[512,512]{1,0:T(8,128)(2,1)}) fusion(bf16[512,512]{1,0:T(8,128)(2,1)} %param.11, bf16[32,16,512]{2,1,0:T(8,128)(2,1)} %all_to_all.25, bf16[512,4096]{1,0:T(8,128)(2,1)} %param.16, bf16[512,4096]{1,0:T(8,128)(2,1)} %all-gather.2.cloned.1.call-done), kind=kOutput, calls=%fused_computation.11 | convolution fusion | flops 2149056512 | bytes 10485760 | tf_op jit(solution)/shard_map/dot_general | solution.py:203
  68.0 14.3 %all_to_all.26.grad_ref = bf16[32,16,512]{2,1,0:T(8,128)(2,1)S(1)} all-to-all(bf16[32,16,512]{2,1,0:T(8,128)(2,1)S(1)} %bitcast.23), channel_id=1, replica_groups=mesh['ctx'=32,'tp'=4] {'ctx'}, dimensions={0} | all-to-all | bytes 1048576 | tf_op jit(solution)/shard_map/all_to_all | solution.py:207
  82.3 0.0 copy-done.3
  82.3 0.0 copy-done.9
  82.4 9.2 %shard_map.155 = (bf16[32,16,512]{2,1,0:T(8,128)(2,1)S(1)}, f32[16,16384]{1,0:T(8,128)}, f32[16,1]{1,0:T(8,128)S(1)}) custom-call(bf16[32,16,512]{2,1,0:T(8,128)(2,1)S(1)} %all_to_all.26.grad_ref, bf16[32,16,512]{2,1,0:T(8,128)(2,1)S(1)} %all-to-all-done.gated_ref, f32[1024,512]{1,0:T(8,128)S(1)} %get-tuple-element.13.taps_spec, f32[1024,512]{1,0:T(8,128)S(1)} %copy-done.1, ...), custom_call_target="tpu_custom_call" | custom-call | tf_op jit(solution)/shard_map/pallas_call | solution.py:213
  91.5 0.8 copy-done.7
  92.3 6.0 %all-to-all-start.3 = ((bf16[32,16,512]{2,1,0:T(8,128)(2,1)}), bf16[32,16,512]{2,1,0:T(8,128)(2,1)S(1)}, u32[]{:S(2)}, u32[]{:S(2)}) async-start(bf16[32,16,512]{2,1,0:T(8,128)(2,1)} %copy-done.7), calls=%async_computation.3 | async-start | bytes 1048576 | tf_op jit(solution)/shard_map/all_to_all | solution.py:225
  98.3 4.9 %fusion = bf16[64,32,8,128]{3,2,1,0:T(8,128)(2,1)S(1)} fusion(bf16[512,4096]{1,0:T(8,128)(2,1)} %all-gather.2.cloned.1.call-done, bf16[512,512]{1,0:T(8,128)(2,1)} %bitcast.22, bf16[512,512]{1,0:T(8,128)(2,1)} %param.11), kind=kOutput, calls=%fused_computation.3 | convolution fusion | flops 2150629376 | bytes 9437184 | tf_op jit(solution)/shard_map/dot_general | solution.py:209
  103.2 3.2 %copy.23 = bf16[64,32,8,128]{3,2,0,1:T(8,128)(2,1)} copy(bf16[64,32,8,128]{3,2,1,0:T(8,128)(2,1)S(1)} %fusion) | data formatting | bytes 8388608 | tf_op jit(solution)/shard_map/reshape | solution.py:210
  106.3 0.7 all-to-all-done.3
  107.1 7.8 %all-to-all-start.4 = ((bf16[32,512,128]{2,1,0:T(8,128)(2,1)}), bf16[32,512,128]{2,1,0:T(8,128)(2,1)}, u32[]{:S(2)}, u32[]{:S(2)}) async-start(bf16[32,512,128]{2,1,0:T(8,128)(2,1)} %bitcast.21), calls=%async_computation.4 | async-start | bytes 8388608 | tf_op jit(solution)/shard_map/all_to_all | solution.py:211
  114.9 0.6 reduce
  115.5 1.2 fusion.4
  116.8 46.4 %all-to-all-done.4 = bf16[32,512,128]{2,1,0:T(8,128)(2,1)} async-done(((bf16[32,512,128]{2,1,0:T(8,128)(2,1)}), bf16[32,512,128]{2,1,0:T(8,128)(2,1)}, u32[]{:S(2)}, u32[]{:S(2)}) %all-to-all-start.4) | async-done | bytes 4194336 | tf_op jit(solution)/shard_map/all_to_all | solution.py:211
  163.2 3.5 %convert_reduce_fusion = f32[512,128]{1,0:T(8,128)} fusion(bf16[32,512,128]{2,1,0:T(8,128)(2,1)} %all-to-all-done.4), kind=kLoop, calls=%fused_computation | loop fusion | flops 4128768 | bytes 4456448 | tf_op jit(solution)/shard_map/reduce_sum | solution.py:212
  (17 shorter events, 0.0 us)
Async XLA Ops:
  7.2 53.8 %all-gather.2.cloned.1.call-start = ((), (), s32[]{:S(2)}) async-start(), calls=%async_computation.5 | async-start | bytes 5242880 | tf_op jit(solution)/shard_map/all_gather | solution.py:180
  10.0 21.5 %all-to-all-start = ((bf16[32,16,512]{2,1,0:T(8,128)(2,1)}), bf16[32,16,512]{2,1,0:T(8,128)(2,1)S(1)}, u32[]{:S(2)}, u32[]{:S(2)}) async-start(bf16[32,16,512]{2,1,0:T(8,128)(2,1)} %bitcast), calls=%async_computation | async-start | bytes 1048576 | tf_op jit(solution)/shard_map/all_to_all | solution.py:192
  31.6 1.0 copy-start.2
  32.6 1.3 copy-start.4
  33.9 0.9 copy-start.5
  34.8 0.8 copy-start.8
  35.6 0.8 copy-start.10
  44.0 1.3 copy-start
  61.0 21.4 %copy-start.3 = (bf16[512,512]{1,0:T(8,128)(2,1)S(1)}, bf16[512,512]{1,0:T(8,128)(2,1)}, u32[]{:S(2)}) copy-start(bf16[512,512]{1,0:T(8,128)(2,1)} %constant.13.clone.second_ref) | copy-start | bytes 1572868
  61.0 21.4 %copy-start.6 = (f32[64,512]{1,0:T(8,128)S(1)}, f32[64,512]{1,0:T(8,128)}, u32[]{:S(2)}) copy-start(f32[64,512]{1,0:T(8,128)} %constant.12.clone.turn_ref) | copy-start | bytes 393220
  61.0 21.4 %copy-start.9 = (bf16[128,192]{1,0:T(8,128)(2,1)S(1)}, bf16[128,192]{1,0:T(8,128)(2,1)}, u32[]{:S(2)}) copy-start(bf16[128,192]{1,0:T(8,128)(2,1)} %constant.10.clone.first_ref) | copy-start | bytes 147460
  61.0 21.4 %copy-start.11 = (bf16[64,256]{1,0:T(8,128)(2,1)S(1)}, bf16[64,256]{1,0:T(8,128)(2,1)}, u32[]{:S(2)}) copy-start(bf16[64,256]{1,0:T(8,128)(2,1)} %constant.11.clone.last_ref) | copy-start | bytes 98308
  61.0 21.3 %copy-start.1 = (f32[1024,512]{1,0:T(8,128)S(1)}, f32[1024,512]{1,0:T(8,128)}, u32[]{:S(2)}) copy-start(f32[1024,512]{1,0:T(8,128)} %copy-done) | copy-start | bytes 6291460
  91.5 0.8 copy-start.7
  92.3 14.8 %all-to-all-start.3 = ((bf16[32,16,512]{2,1,0:T(8,128)(2,1)}), bf16[32,16,512]{2,1,0:T(8,128)(2,1)S(1)}, u32[]{:S(2)}, u32[]{:S(2)}) async-start(bf16[32,16,512]{2,1,0:T(8,128)(2,1)} %copy-done.7), calls=%async_computation.3 | async-start | bytes 1048576 | tf_op jit(solution)/shard_map/all_to_all | solution.py:225
  107.1 8.5 %copy-start.12 = (bf16[512,512]{1,0:T(8,128)(2,1)S(1)}, bf16[512,512]{1,0:T(8,128)(2,1)}, u32[]{:S(2)}) copy-start(bf16[512,512]{1,0:T(8,128)(2,1)} %param.13) | copy-start | bytes 1572868
  107.1 8.5 %copy-start.13 = (bf16[512,512]{1,0:T(8,128)(2,1)S(1)}, bf16[512,512]{1,0:T(8,128)(2,1)}, u32[]{:S(2)}) copy-start(bf16[512,512]{1,0:T(8,128)(2,1)} %param.12) | copy-start | bytes 1572868
  107.1 56.1 %all-to-all-start.4 = ((bf16[32,512,128]{2,1,0:T(8,128)(2,1)}), bf16[32,512,128]{2,1,0:T(8,128)(2,1)}, u32[]{:S(2)}, u32[]{:S(2)}) async-start(bf16[32,512,128]{2,1,0:T(8,128)(2,1)} %bitcast.21), calls=%async_computation.4 | async-start | bytes 8388608 | tf_op jit(solution)/shard_map/all_to_all | solution.py:211
Sparse Core Ops, SparseCore 0:
  9.7 41.0 all-gather.1
where the time goes:
time: 174 us
  waiting for transfers between devices  59.2 us (34%)
  blocking collectives  29.9 us (17%)
  starting transfers between devices  23.3 us (13%)
  Pallas kernels  16.8 us (10%)
  between operations  14.1 us (8%)
  matrix products  11.9 us (7%)
  local copies, waits for them, and re-layouts  10.9 us (6%)
  other arithmetic  7.49 us (4%)
    all_to_all x1, waiting for transfers between devices, body(): terms = lax.all_to_all(terms, 'ctx', split_axis=0, concat_axis=0)  46.4 us
    all_to_all x1, blocking collectives, body(): lax.all_to_all(conv_chan, 'ctx', split_axis=0, concat_axis=0)  15.6 us
    all_to_all x1, blocking collectives, body(): lax.all_to_all(grad_conv.reshape(blocks), 'ctx', split_axis=0, concat_axi...  14.3 us
    all_to_all x1, waiting for transfers between devices, body(): lax.all_to_all(gated.reshape(blocks), 'ctx', split_axis=0, concat_axis=0)  11.3 us
    all_to_all x1, starting transfers between devices, body(): lax.all_to_all(gated.reshape(blocks), 'ctx', split_axis=0, concat_axis=0)  9.45 us
    pallas_call x1, Pallas kernels, body(): pl.pallas_call(grad_kernel, out_shape=(jax.ShapeDtypeStruct(blocks, jnp.b...  9.17 us
    all_to_all x1, starting transfers between devices, body(): terms = lax.all_to_all(terms, 'ctx', split_axis=0, concat_axis=0)  7.84 us
    pallas_call x1, Pallas kernels, body(): pl.pallas_call(conv_kernel, out_shape=(jax.ShapeDtypeStruct(blocks, jnp.b...  7.64 us
  transfers between devices with their start and end apart: 4, of which 3 were waited for; matrix products, arithmetic and copies ran while one was open for 7% of the time, Pallas kernels for 4%

commit v1 on v0

--- a/solution.py
+++ b/solution.py
@@ -12,6 +12,8 @@
 LANES = 128
 CHANS = 16
 SEQ_BLOCKS = 32
+COT_CHUNKS = 4
+COT_ROWS = 128
 
 
 def bf16_pair(values):
@@ -130,104 +132,356 @@
     lax.fori_loop(0, SEQ_BLOCKS, step, 0, unroll=4)
 
 
-def conv_kernel(
-    gated_ref, taps_ref, skip_ref, first_ref, last_ref, turn_ref, second_ref,
-    conv_ref, taps_spec, gated_spec, grid, mixed, spec,
-):
+def taps_to_grid(taps, skip_ref, grid):
     for a in range(ROWS):
         for half in range(2):
             start = a * COLS + half * LANES
-            grid[half, a * CHANS : (a + 1) * CHANS, :] = taps_ref[:, start : start + LANES]
+            grid[half, a * CHANS : (a + 1) * CHANS, :] = taps[:, start : start + LANES]
+    row = lax.broadcasted_iota(jnp.int32, (CHANS, CHANS), 0)
+    col = lax.broadcasted_iota(jnp.int32, (CHANS, CHANS), 1)
+    skip = jnp.sum(jnp.where(row == col, skip_ref[...], 0.0), axis=1, keepdims=True)
     lane = lax.broadcasted_iota(jnp.int32, (CHANS, LANES), 1)
-    grid[0, :CHANS, :] += jnp.where(lane == 0, skip_ref[...], 0.0)
-    spectrum_of(grid, first_ref, turn_ref, second_ref, mixed, taps_spec, True)
-    take_blocks(gated_ref, grid)
-    spectrum_of(grid, first_ref, turn_ref, second_ref, mixed, gated_spec, False)
-    product_to(mixed, taps_spec, gated_spec, False)
-    signal_of(mixed, last_ref, turn_ref, second_ref, spec, grid)
-    give_blocks(grid, conv_ref)
-
-
-def grad_kernel(
-    grad_ref, gated_ref, taps_spec, gated_spec, first_ref, last_ref, turn_ref, second_ref,
-    back_ref, taps_grad_ref, skip_grad_ref, grid, mixed, spec, grad_spec,
-):
-    take_blocks(grad_ref, grid)
-    spectrum_of(grid, first_ref, turn_ref, second_ref, mixed, grad_spec, False)
-    product_to(mixed, taps_spec, grad_spec, True)
-    signal_of(mixed, last_ref, turn_ref, second_ref, spec, grid)
-    give_blocks(grid, back_ref)
-    product_to(mixed, gated_spec, grad_spec, True)
-    signal_of(mixed, last_ref, turn_ref, second_ref, spec, grid)
+    grid[0, :CHANS, :] += jnp.where(lane == 0, skip, 0.0)
+
+
+def grid_to_taps(grid, taps):
     for a in range(ROWS):
         for half in range(2):
             start = a * COLS + half * LANES
-            taps_grad_ref[:, start : start + LANES] = grid[half, a * CHANS : (a + 1) * CHANS, :]
-
+            taps[:, start : start + LANES] = grid[half, a * CHANS : (a + 1) * CHANS, :]
+
+
+def skip_gradient(grad, gated, out_ref):
     def step(s, total):
-        return total + grad_ref[s].astype(jnp.float32) * gated_ref[s].astype(jnp.float32)
+        return total + grad[s].astype(jnp.float32) * gated[s].astype(jnp.float32)
 
     total = lax.fori_loop(0, SEQ_BLOCKS, step, jnp.zeros((CHANS, 2 * COLS), jnp.float32))
-    skip_grad_ref[...] = jnp.sum(total, axis=1, keepdims=True)
-
-
-def vmem_specs(count):
-    return [pl.BlockSpec(memory_space=pltpu.VMEM)] * count
+    total = jnp.sum(total, axis=1, keepdims=True)
+    row = lax.broadcasted_iota(jnp.int32, (CHANS, CHANS), 0)
+    col = lax.broadcasted_iota(jnp.int32, (CHANS, CHANS), 1)
+    out_ref[...] = jnp.sum(jnp.where(row == col, total, 0.0), axis=0, keepdims=True)
+
+
+def for_blocks(step, unroll=4):
+    def body(s, carry):
+        step(s)
+        return carry
+
+    lax.fori_loop(0, SEQ_BLOCKS, body, 0, unroll=unroll)
+
+
+def block_rows(s):
+    return pl.ds(pl.multiple_of(s * CHANS, CHANS), CHANS)
+
+
+def kernel(
+    query_in, key_in, value_in, taps_in, skip_ref, weight_in, cot_in, first_in, last_in, turn_in, second_in,
+    query_out, key_out, value_out, taps_out, skip_out, weight_out,
+    query, key, value, taps, weight, first, last, turn, second,
+    cot, gated, gated_got, conv, conv_got, grad, grad_got, back, back_got, terms, terms_got, grad_mixed, gate_mixed,
+    grid, mixed, spec, taps_spec, gated_spec, grad_spec, query_res, key_res, value_res, taps_res, weight_res,
+    load_sem, store_sem, gated_sems, conv_sems, grad_sems, back_sems, terms_sems, near_sems, far_sems, relay_sems,
+):
+    me = lax.axis_index("ctx")
+    part = lax.axis_index("tp")
+    sibling = part + 1 - 2 * (part % 2)
+    across = (part + 2) % 4
+    diagonal = (sibling + 2) % 4
+
+    def load(index, source, target):
+        copy = pltpu.make_async_copy(source, target, load_sem.at[index])
+        copy.start()
+        return copy
+
+    key_load = load(0, key_in, key)
+    value_load = load(1, value_in, value)
+    cot_load = load(2, cot_in, cot.at[part])
+    first_load = load(3, first_in, first)
+    turn_load = load(4, turn_in, turn)
+    second_load = load(5, second_in, second)
+    taps_load = load(6, taps_in, taps)
+    last_load = load(7, last_in, last)
+    weight_load = load(8, weight_in, weight)
+    query_load = load(9, query_in, query)
+
+    barrier = pltpu.get_barrier_semaphore()
+
+    def greet(i, carry):
+        pl.semaphore_signal(
+            barrier, inc=1, device_id={"ctx": (me + i) % SEQ_BLOCKS}, device_id_type=pl.DeviceIdType.MESH
+        )
+        return carry
+
+    lax.fori_loop(1, SEQ_BLOCKS, greet, 0)
+    for other in (sibling, across):
+        pl.semaphore_signal(barrier, inc=1, device_id={"tp": other}, device_id_type=pl.DeviceIdType.MESH)
+
+    key_load.wait()
+    value_load.wait()
+
+    def gate(s):
+        gated[s] = (key[s].astype(jnp.float32) * value[s].astype(jnp.float32)).astype(jnp.bfloat16)
+
+    for_blocks(gate)
+    pl.semaphore_wait(barrier, SEQ_BLOCKS + 1)
+
+    def to_peer(source, target, sems, peer, slot):
+        return pltpu.make_async_remote_copy(
+            src_ref=source.at[peer],
+            dst_ref=target.at[slot],
+            send_sem=sems.at[0, peer],
+            recv_sem=sems.at[1, slot],
+            device_id={"ctx": peer},
+            device_id_type=pl.DeviceIdType.MESH,
+        )
+
+    def exchange(source, target, sems):
+        def step(i, carry):
+            to_peer(source, target, sems, (me + i) % SEQ_BLOCKS, me).start()
+            return carry
+
+        lax.fori_loop(1, SEQ_BLOCKS, step, 0)
+        target[me] = source[me]
+
+    def arrived(source, target, sems):
+        def step(i, carry):
+            peer = (me + SEQ_BLOCKS - i) % SEQ_BLOCKS
+            to_peer(source, target, sems, peer, peer).wait_recv()
+            return carry
+
+        lax.fori_loop(1, SEQ_BLOCKS, step, 0)
+
+    def sent(source, target, sems):
+        def step(i, carry):
+            to_peer(source, target, sems, (me + i) % SEQ_BLOCKS, me).wait_send()
+            return carry
+
+        lax.fori_loop(1, SEQ_BLOCKS, step, 0)
+
+    exchange(gated, gated_got, gated_sems)
+
+    near = pltpu.make_async_remote_copy(
+        src_ref=cot_in,
+        dst_ref=cot.at[part],
+        send_sem=near_sems.at[0],
+        recv_sem=near_sems.at[1],
+        device_id={"tp": sibling},
+        device_id_type=pl.DeviceIdType.MESH,
+    )
+    near.start()
+
+    def chunk_rows(j):
+        return pl.ds(j * COT_ROWS, COT_ROWS)
+
+    def far(j):
+        return pltpu.make_async_remote_copy(
+            src_ref=cot_in.at[chunk_rows(j)],
+            dst_ref=cot.at[part, chunk_rows(j)],
+            send_sem=far_sems.at[0, j],
+            recv_sem=far_sems.at[1, j],
+            device_id={"tp": across},
+            device_id_type=pl.DeviceIdType.MESH,
+        )
+
+    def relay(j):
+        return pltpu.make_async_remote_copy(
+            src_ref=cot.at[across, chunk_rows(j)],
+            dst_ref=cot.at[across, chunk_rows(j)],
+            send_sem=relay_sems.at[0, j],
+            recv_sem=relay_sems.at[1, j],
+            device_id={"tp": sibling},
+            device_id_type=pl.DeviceIdType.MESH,
+        )
+
+    for j in range(COT_CHUNKS):
+        far(j).start()
+
+    taps_load.wait()
+    first_load.wait()
+    turn_load.wait()
+    second_load.wait()
+    taps_to_grid(taps, skip_ref, grid)
+    spectrum_of(grid, first, turn, second, mixed, taps_spec, True)
+
+    def mix_features(p, fresh):
+        def step(i, carry):
+            rows = pl.ds(pl.multiple_of(i * 256, 256), 256)
+            columns = pl.ds(pl.multiple_of(p * 1024, 1024), 1024)
+            term = lax.dot_general(
+                weight[:, columns], cot[p, rows, :], (((1,), (1,)), ((), ())),
+                preferred_element_type=jnp.float32,
+            )
+            if fresh:
+                grad_mixed[:, rows] = term
+            else:
+                grad_mixed[:, rows] += term
+            return carry
+
+        lax.fori_loop(0, 2, step, 0)
+
+    cot_load.wait()
+    weight_load.wait()
+    mix_features(part, True)
+    last_load.wait()
+    query_load.wait()
+
+    arrived(gated, gated_got, gated_sems)
+    take_blocks(gated_got, grid)
+    spectrum_of(grid, first, turn, second, mixed, gated_spec, False)
+    product_to(mixed, taps_spec, gated_spec, False)
+    signal_of(mixed, last, turn, second, spec, grid)
+    give_blocks(grid, conv)
+    exchange(conv, conv_got, conv_sems)
+
+    near.wait_recv()
+    mix_features(sibling, False)
+    for j in range(COT_CHUNKS):
+        far(j).wait_recv()
+        relay(j).start()
+    mix_features(across, False)
+    for j in range(COT_CHUNKS):
+        relay(j).wait_recv()
+    mix_features(diagonal, False)
+
+    def cotangent(s):
+        grad[s] = (grad_mixed[block_rows(s), :] * query[s].astype(jnp.float32)).astype(jnp.bfloat16)
+
+    for_blocks(cotangent)
+    exchange(grad, grad_got, grad_sems)
+
+    arrived(conv, conv_got, conv_sems)
+
+    def gate_output(s):
+        conv_f = conv_got[s].astype(jnp.float32)
+        gate_mixed[block_rows(s), :] = (query[s].astype(jnp.float32) * conv_f).astype(jnp.bfloat16)
+        query_res[s] = (grad_mixed[block_rows(s), :] * conv_f).astype(jnp.bfloat16)
+
+    for_blocks(gate_output)
+    query_store = pltpu.make_async_copy(query_res, query_out, store_sem.at[0])
+    query_store.start()
+
+    def term_step(i, carry):
+        pair = (me // 2 + 1 + i) % (SEQ_BLOCKS // 2)
+        columns = pl.ds(pl.multiple_of(pair % 4 * 256, 256), 256)
+        term = dot(gate_mixed[...], cot[pair // 4, :, columns]).astype(jnp.bfloat16)
+        for half in range(2):
+            peer = pair * 2 + half
+            terms[peer] = term[:, half * LANES : (half + 1) * LANES]
+
+            @pl.when(peer != me)
+            def _():
+                to_peer(terms, terms_got, terms_sems, peer, me).start()
+
+        return carry
+
+    lax.fori_loop(0, SEQ_BLOCKS // 2, term_step, 0)
+
+    arrived(grad, grad_got, grad_sems)
+    take_blocks(grad_got, grid)
+    spectrum_of(grid, first, turn, second, mixed, grad_spec, False)
+    product_to(mixed, taps_spec, grad_spec, True)
+    signal_of(mixed, last, turn, second, spec, grid)
+    give_blocks(grid, back)
+    exchange(back, back_got, back_sems)
+    product_to(mixed, gated_spec, grad_spec, True)
+    signal_of(mixed, last, turn, second, spec, grid)
+    grid_to_taps(grid, taps_res)
+    taps_store = pltpu.make_async_copy(taps_res, taps_out, store_sem.at[1])
+    taps_store.start()
+    skip_gradient(grad_got, gated_got, skip_out)
+
+    weight_res[...] = terms[me].astype(jnp.float32)
+
+    def sum_step(i, carry):
+        peer = (me + SEQ_BLOCKS - i) % SEQ_BLOCKS
+        to_peer(terms, terms_got, terms_sems, peer, peer).wait_recv()
+        weight_res[...] += terms_got[peer].astype(jnp.float32)
+        return carry
+
+    arrived(back, back_got, back_sems)
+
+    def gate_input(s):
+        back_f = back_got[s].astype(jnp.float32)
+        key_res[s] = (back_f * value[s].astype(jnp.float32)).astype(jnp.bfloat16)
+        value_res[s] = (back_f * key[s].astype(jnp.float32)).astype(jnp.bfloat16)
+
+    for_blocks(gate_input)
+    key_store = pltpu.make_async_copy(key_res, key_out, store_sem.at[2])
+    key_store.start()
+    value_store = pltpu.make_async_copy(value_res, value_out, store_sem.at[3])
+    value_store.start()
+    lax.fori_loop(1, SEQ_BLOCKS, sum_step, 0)
+    weight_store = pltpu.make_async_copy(weight_res, weight_out, store_sem.at[4])
+    weight_store.start()
+
+    sent(gated, gated_got, gated_sems)
+    sent(conv, conv_got, conv_sems)
+    sent(grad, grad_got, grad_sems)
+    sent(back, back_got, back_sems)
+    sent(terms, terms_got, terms_sems)
+    near.wait_send()
+    for j in range(COT_CHUNKS):
+        far(j).wait_send()
+        relay(j).wait_send()
+    for copy in (query_store, taps_store, key_store, value_store, weight_store):
+        copy.wait()
 
 
 def body(query_gate, key_branch, value_branch, filter_taps, skip_gain, out_weight, out_grad):
-    first, last, turn, second = [jnp.asarray(t) for t in tables()]
-    full_grad = lax.all_gather(out_grad, "tp", axis=1, tiled=True)
-    query_f = query_gate.astype(jnp.float32)
-    key_f = key_branch.astype(jnp.float32)
-    value_f = value_branch.astype(jnp.float32)
+    constants = [jnp.asarray(t) for t in tables()]
     blocks = (SEQ_BLOCKS, CHANS, 2 * COLS)
-    spec_shape = jax.ShapeDtypeStruct((CHANS * ROWS, 2 * COLS), jnp.float32)
-    grid = pltpu.VMEM((2, CHANS * ROWS, LANES), jnp.float32)
-    mixed_s = pltpu.VMEM((CHANS * ROWS, 2 * COLS), jnp.bfloat16)
-    spec_s = pltpu.VMEM((CHANS * ROWS, 2 * COLS), jnp.float32)
-    params = pltpu.CompilerParams(vmem_limit_bytes=40 * 1024 * 1024)
-
-    gated = (key_f * value_f).astype(jnp.bfloat16)
-    gated_chan = lax.all_to_all(gated.reshape(blocks), "ctx", split_axis=0, concat_axis=0)
-    conv_chan, taps_spec, gated_spec = pl.pallas_call(
-        conv_kernel,
-        out_shape=(jax.ShapeDtypeStruct(blocks, jnp.bfloat16), spec_shape, spec_shape),
-        in_specs=vmem_specs(7),
-        out_specs=vmem_specs(3),
-        scratch_shapes=[grid, mixed_s, spec_s],
-        compiler_params=params,
-    )(gated_chan, filter_taps, skip_gain[:, None], first, last, turn, second)
-    conv_out = lax.all_to_all(conv_chan, "ctx", split_axis=0, concat_axis=0).reshape(query_gate.shape)
-    conv_f = conv_out.astype(jnp.float32)
-    grad_mixed = lax.dot_general(
-        out_weight, full_grad, (((1,), (1,)), ((), ())), preferred_element_type=jnp.float32
+    bf16, f32 = jnp.bfloat16, jnp.float32
+    in_hbm = pl.BlockSpec(memory_space=pl.ANY)
+    in_vmem = pl.BlockSpec(memory_space=pltpu.VMEM)
+    block_buffer = pltpu.VMEM(blocks, bf16)
+    spec_buffer = pltpu.VMEM((CHANS * ROWS, 2 * COLS), f32)
+    terms_buffer = pltpu.VMEM((SEQ_BLOCKS, 512, LANES), bf16)
+    peer_sems = pltpu.SemaphoreType.DMA((2, SEQ_BLOCKS))
+    dma = pltpu.SemaphoreType.DMA
+    grad_query, grad_key, grad_value, grad_filter, grad_skip, grad_weight = pl.pallas_call(
+        kernel,
+        out_shape=(
+            jax.ShapeDtypeStruct(blocks, bf16),
+            jax.ShapeDtypeStruct(blocks, bf16),
+            jax.ShapeDtypeStruct(blocks, bf16),
+            jax.ShapeDtypeStruct(filter_taps.shape, f32),
+            jax.ShapeDtypeStruct((1, CHANS), f32),
+            jax.ShapeDtypeStruct((512, LANES), f32),
+        ),
+        in_specs=[in_hbm] * 4 + [in_vmem] + [in_hbm] * 6,
+        out_specs=[in_hbm] * 4 + [in_vmem, in_hbm],
+        scratch_shapes=[
+            block_buffer, block_buffer, block_buffer,
+            pltpu.VMEM(filter_taps.shape, f32),
+            pltpu.VMEM(out_weight.shape, bf16),
+            *[pltpu.VMEM(t.shape, t.dtype) for t in constants],
+            pltpu.VMEM((4, 512, 1024), bf16),
+            *[block_buffer] * 8,
+            terms_buffer, terms_buffer,
+            pltpu.VMEM((512, 512), f32),
+            pltpu.VMEM((512, 512), bf16),
+            pltpu.VMEM((2, CHANS * ROWS, LANES), f32),
+            pltpu.VMEM((CHANS * ROWS, 2 * COLS), bf16),
+            *[spec_buffer] * 4,
+            block_buffer, block_buffer, block_buffer,
+            pltpu.VMEM(filter_taps.shape, f32),
+            pltpu.VMEM((512, LANES), f32),
+            dma((10,)), dma((5,)),
+            *[peer_sems] * 5,
+            dma((2,)), dma((2, COT_CHUNKS)), dma((2, COT_CHUNKS)),
+        ],
+        compiler_params=pltpu.CompilerParams(
+            collective_id=0, has_side_effects=True, vmem_limit_bytes=56 * 1024 * 1024
+        ),
+    )(
+        query_gate.reshape(blocks), key_branch.reshape(blocks), value_branch.reshape(blocks), filter_taps,
+        skip_gain[None, :], out_weight, out_grad, *constants,
     )
-    grad_conv = (grad_mixed * query_f).astype(jnp.bfloat16)
-    grad_chan = lax.all_to_all(grad_conv.reshape(blocks), "ctx", split_axis=0, concat_axis=0)
-    mixed = (query_f * conv_f).astype(jnp.bfloat16)
-    terms = lax.dot_general(mixed, full_grad, (((1,), (0,)), ((), ())), preferred_element_type=jnp.float32)
-    terms = terms.astype(jnp.bfloat16).reshape(terms.shape[0], SEQ_BLOCKS, -1).transpose(1, 0, 2)
-    terms = lax.all_to_all(terms, "ctx", split_axis=0, concat_axis=0)
-    grad_weight = jnp.sum(terms.astype(jnp.float32), axis=0)
-    back_chan, grad_filter, grad_skip = pl.pallas_call(
-        grad_kernel,
-        out_shape=(
-            jax.ShapeDtypeStruct(blocks, jnp.bfloat16),
-            jax.ShapeDtypeStruct(filter_taps.shape, jnp.float32),
-            jax.ShapeDtypeStruct((CHANS, 1), jnp.float32),
-        ),
-        in_specs=vmem_specs(8),
-        out_specs=vmem_specs(3),
-        scratch_shapes=[grid, mixed_s, spec_s, spec_s],
-        compiler_params=params,
-    )(grad_chan, gated_chan, taps_spec, gated_spec, first, last, turn, second)
-    grad_gated = lax.all_to_all(back_chan, "ctx", split_axis=0, concat_axis=0).reshape(query_gate.shape)
-    grad_query = (grad_mixed * conv_f).astype(jnp.bfloat16)
-    grad_gated_f = grad_gated.astype(jnp.float32)
-    grad_key = (grad_gated_f * value_f).astype(jnp.bfloat16)
-    grad_value = (grad_gated_f * key_f).astype(jnp.bfloat16)
-    return (grad_query, grad_key, grad_value, grad_filter, grad_skip[:, 0], grad_weight)
+    shape = query_gate.shape
+    return (
+        grad_query.reshape(shape), grad_key.reshape(shape), grad_value.reshape(shape),
+        grad_filter, grad_skip[0], grad_weight,
+    )
 
 
 def solution(mesh):

time: 174 us -> 146 us (0.84)
  the two profiles are of different devices: /device:TPU:14 before, /device:TPU:1 now
where the time goes in v1:
time: 146 us
  Pallas kernels  136 us (93%)
  local copies, waits for them, and re-layouts  9.13 us (6%)
    pallas_call x1, Pallas kernels, body(): pl.pallas_call(kernel, out_shape=(jax.ShapeDtypeStruct(blocks, bf16), jax...  136 us
    unnamed x10, local copies, waits for them, and re-layouts  9.13 us

profile of v1, /device:TPU:1, one launch (start us, length us, event | category | flops | bytes accessed | tf_op | source)
XLA Modules:
  0.0 145.9 jit_solution(11243920250947846811)
XLA Ops:
  0.6 136.1 %shard_map.154 = (bf16[32,16,512]{2,1,0:T(8,128)(2,1)}, bf16[32,16,512]{2,1,0:T(8,128)(2,1)}, bf16[32,16,512]{2,1,0:T(8,128)(2,1)}, f32[16,16384]{1,0:T(8,128)}, f32[1,16]{1,0:T(1,128)}, /*index=5*/f32[512,128]{1,0:T(8,128)}) custom-call(bf16[32,16,512]{2,1,0:T(8,128)(2,1)} %bitcast.8, bf16[32,16,512]{2,1,0:T(8,128)(2,1)} %bitcast.9, ...), custom_call_target="tpu_custom_call" | custom-call | tf_op jit(solution)/shard_map/pallas_call | solution.py:441
  136.8 0.0 copy-start.1
  136.8 0.0 copy-start
  136.8 1.9 %copy.23 = bf16[512,512]{1,0:T(8,128)(2,1)} copy(bf16[512,512]{1,0:T(8,128)(2,1)} %bitcast.13) | data formatting | bytes 1048576
  138.7 1.9 %copy.24 = bf16[512,512]{1,0:T(8,128)(2,1)} copy(bf16[512,512]{1,0:T(8,128)(2,1)} %bitcast.12) | data formatting | bytes 1048576
  140.6 1.9 %copy.25 = bf16[512,512]{1,0:T(8,128)(2,1)} copy(bf16[512,512]{1,0:T(8,128)(2,1)} %bitcast.11) | data formatting | bytes 1048576
  142.4 2.3 %copy.26 = f32[16,16384]{1,0:T(8,128)} copy(f32[16,16384]{1,0:T(8,128)} %get-tuple-element.27) | data formatting | bytes 2097152
  144.7 0.0 copy-done.1
  144.7 0.5 copy.27
  145.2 0.0 copy-done
  145.2 0.7 copy.28
Async XLA Ops:
  136.8 7.9 %copy-start.1 = (f32[1,16]{1,0:T(1,128)S(1)}, f32[1,16]{1,0:T(1,128)}, u32[]{:S(2)}) copy-start(f32[1,16]{1,0:T(1,128)} %get-tuple-element.16) | copy-start | bytes 196
  136.8 8.4 %copy-start = (f32[512,128]{1,0:T(8,128)S(1)}, f32[512,128]{1,0:T(8,128)}, u32[]{:S(2)}) copy-start(f32[512,128]{1,0:T(8,128)} %get-tuple-element.29) | copy-start | bytes 786436

commit v2 on v1

--- a/solution.py
+++ b/solution.py
@@ -14,6 +14,8 @@
 SEQ_BLOCKS = 32
 COT_CHUNKS = 4
 COT_ROWS = 128
+TERM_CHUNKS = 2
+TERM_ROWS = 256 // TERM_CHUNKS
 
 
 def bf16_pair(values):
@@ -36,7 +38,7 @@
     phase_b = 2.0 * np.pi * (np.outer(np.arange(COLS), np.arange(COLS)) % COLS) / COLS
     cos_b, sin_b = np.cos(phase_b), np.sin(phase_b)
     second = np.block([[cos_b, -sin_b], [sin_b, cos_b]]).astype(ml_dtypes.bfloat16)
-    return first, last, turn, second
+    return [t.astype(np.float32) for t in (first, last, turn, second)]
 
 
 def dot(left, right):
@@ -177,10 +179,11 @@
 def kernel(
     query_in, key_in, value_in, taps_in, skip_ref, weight_in, cot_in, first_in, last_in, turn_in, second_in,
     query_out, key_out, value_out, taps_out, skip_out, weight_out,
-    query, key, value, taps, weight, first, last, turn, second,
-    cot, gated, gated_got, conv, conv_got, grad, grad_got, back, back_got, terms, terms_got, grad_mixed, gate_mixed,
+    query, key, value, taps, weight, first_wide, last_wide, turn, second_wide, first, last, second,
+    cot, gated, gated_got, conv, conv_got, grad, grad_got, back, back_got, terms, terms_got,
+    second_terms, second_got, third, third_got, grad_mixed, gate_mixed,
     grid, mixed, spec, taps_spec, gated_spec, grad_spec, query_res, key_res, value_res, taps_res, weight_res,
-    load_sem, store_sem, gated_sems, conv_sems, grad_sems, back_sems, terms_sems, near_sems, far_sems, relay_sems,
+    load_sem, store_sem, gated_sems, conv_sems, grad_sems, back_sems, terms_sems, second_sems, third_sems, near_sems, far_sems, relay_sems,
 ):
     me = lax.axis_index("ctx")
     part = lax.axis_index("tp")
@@ -196,11 +199,11 @@
     key_load = load(0, key_in, key)
     value_load = load(1, value_in, value)
     cot_load = load(2, cot_in, cot.at[part])
-    first_load = load(3, first_in, first)
+    first_load = load(3, first_in, first_wide)
     turn_load = load(4, turn_in, turn)
-    second_load = load(5, second_in, second)
+    second_load = load(5, second_in, second_wide)
     taps_load = load(6, taps_in, taps)
-    last_load = load(7, last_in, last)
+    last_load = load(7, last_in, last_wide)
     weight_load = load(8, weight_in, weight)
     query_load = load(9, query_in, query)
 
@@ -225,38 +228,34 @@
     for_blocks(gate)
     pl.semaphore_wait(barrier, SEQ_BLOCKS + 1)
 
-    def to_peer(source, target, sems, peer, slot):
+    def to_device(source, target, send_sem, recv_sem, device):
         return pltpu.make_async_remote_copy(
-            src_ref=source.at[peer],
-            dst_ref=target.at[slot],
-            send_sem=sems.at[0, peer],
-            recv_sem=sems.at[1, slot],
-            device_id={"ctx": peer},
+            src_ref=source,
+            dst_ref=target,
+            send_sem=send_sem,
+            recv_sem=recv_sem,
+            device_id=device,
             device_id_type=pl.DeviceIdType.MESH,
         )
 
     def exchange(source, target, sems):
         def step(i, carry):
-            to_peer(source, target, sems, (me + i) % SEQ_BLOCKS, me).start()
+            peer = (me + i) % SEQ_BLOCKS
+            to_device(source.at[peer], target.at[me], sems.at[0], sems.at[1], {"ctx": peer}).start()
             return carry
 
         lax.fori_loop(1, SEQ_BLOCKS, step, 0)
         target[me] = source[me]
 
+    def whole_exchange(source, target, sems):
+        blocks = pl.ds(0, SEQ_BLOCKS - 1)
+        return to_device(source.at[blocks], target.at[blocks], sems.at[0], sems.at[1], {"tp": across})
+
     def arrived(source, target, sems):
-        def step(i, carry):
-            peer = (me + SEQ_BLOCKS - i) % SEQ_BLOCKS
-            to_peer(source, target, sems, peer, peer).wait_recv()
-            return carry
-
-        lax.fori_loop(1, SEQ_BLOCKS, step, 0)
+        whole_exchange(source, target, sems).wait_recv()
 
     def sent(source, target, sems):
-        def step(i, carry):
-            to_peer(source, target, sems, (me + i) % SEQ_BLOCKS, me).wait_send()
-            return carry
-
-        lax.fori_loop(1, SEQ_BLOCKS, step, 0)
+        whole_exchange(source, target, sems).wait_send()
 
     exchange(gated, gated_got, gated_sems)
 
@@ -300,6 +299,8 @@
     first_load.wait()
     turn_load.wait()
     second_load.wait()
+    first[...] = first_wide[...].astype(jnp.bfloat16)
+    second[...] = second_wide[...].astype(jnp.bfloat16)
     taps_to_grid(taps, skip_ref, grid)
     spectrum_of(grid, first, turn, second, mixed, taps_spec, True)
 
@@ -323,6 +324,7 @@
     weight_load.wait()
     mix_features(part, True)
     last_load.wait()
+    last[...] = last_wide[...].astype(jnp.bfloat16)
     query_load.wait()
 
     arrived(gated, gated_got, gated_sems)
@@ -335,6 +337,14 @@
 
     near.wait_recv()
     mix_features(sibling, False)
+    arrived(conv, conv_got, conv_sems)
+
+    def gate_output(s):
+        gate_mixed[block_rows(s), :] = (
+            query[s].astype(jnp.float32) * conv_got[s].astype(jnp.float32)
+        ).astype(jnp.bfloat16)
+
+    for_blocks(gate_output)
     for j in range(COT_CHUNKS):
         far(j).wait_recv()
         relay(j).start()
@@ -349,32 +359,68 @@
     for_blocks(cotangent)
     exchange(grad, grad_got, grad_sems)
 
-    arrived(conv, conv_got, conv_sems)
-
-    def gate_output(s):
-        conv_f = conv_got[s].astype(jnp.float32)
-        gate_mixed[block_rows(s), :] = (query[s].astype(jnp.float32) * conv_f).astype(jnp.bfloat16)
-        query_res[s] = (grad_mixed[block_rows(s), :] * conv_f).astype(jnp.bfloat16)
-
-    for_blocks(gate_output)
+    z, y, x = me // 8, me // 2 % 4, me % 2
+
+    def z_peer(k):
+        return (z + k) % 4
+
+    def y_peer(k):
+        return (y + k) % 4
+
+    def peer_of(half, stage, k):
+        if half == stage:
+            return z_peer(k), {"ctx": z_peer(k) * 8 + y * 2 + x}, z
+        return y_peer(k), {"ctx": z * 8 + y_peer(k) * 2 + x}, y
+
+    def term_rows(j):
+        return pl.ds(pl.multiple_of(j * TERM_ROWS, TERM_ROWS), TERM_ROWS)
+
+    def one_of(half, stage, source, target, sems, j, k):
+        place, device, own = peer_of(half, stage, k)
+        return to_device(
+            source.at[half, place, term_rows(j)], target.at[half, own, term_rows(j)],
+            sems.at[0, half, j, k - 1], sems.at[1, half, j, k - 1], device,
+        )
+
+    def side_of(half, j):
+        return to_device(
+            third.at[half, term_rows(j)], third_got.at[half, term_rows(j)],
+            third_sems.at[0, half, j], third_sems.at[1, half, j], {"ctx": me + 1 - 2 * x},
+        )
+
+    def from_peer(half, stage, source, target, sems, j, k):
+        place, device, own = peer_of(half, stage, 4 - k)
+        return to_device(
+            source.at[half, place, term_rows(j)], target.at[half, place, term_rows(j)],
+            sems.at[0, half, j, k - 1], sems.at[1, half, j, k - 1], device,
+        )
+
+    def term_chunk(j):
+        def step(i, carry):
+            p, q = i // 4, i % 4
+            columns = pl.ds(pl.multiple_of(q * 256, 256), 256)
+            targets = pl.ds(pl.multiple_of(p * 256, 256), 256)
+            lower = pl.ds(pl.multiple_of(256 + j * TERM_ROWS, TERM_ROWS), TERM_ROWS)
+            left = jnp.concatenate([gate_mixed[term_rows(j), :], gate_mixed[lower, :]], axis=0)
+            term = dot(left, cot[p, :, columns]).astype(jnp.bfloat16)
+            terms[0, p, term_rows(j), columns] = term[:TERM_ROWS]
+            terms[1, q, term_rows(j), targets] = term[TERM_ROWS:]
+            return carry
+
+        lax.fori_loop(0, 16, step, 0)
+        for k in (2, 1, 3):
+            for half in range(2):
+                one_of(half, 0, terms, terms_got, terms_sems, j, k).start()
+
+    for j in range(TERM_CHUNKS):
+        term_chunk(j)
+
+    def query_gradient(s):
+        query_res[s] = (grad_mixed[block_rows(s), :] * conv_got[s].astype(jnp.float32)).astype(jnp.bfloat16)
+
+    for_blocks(query_gradient)
     query_store = pltpu.make_async_copy(query_res, query_out, store_sem.at[0])
     query_store.start()
-
-    def term_step(i, carry):
-        pair = (me // 2 + 1 + i) % (SEQ_BLOCKS // 2)
-        columns = pl.ds(pl.multiple_of(pair % 4 * 256, 256), 256)
-        term = dot(gate_mixed[...], cot[pair // 4, :, columns]).astype(jnp.bfloat16)
-        for half in range(2):
-            peer = pair * 2 + half
-            terms[peer] = term[:, half * LANES : (half + 1) * LANES]
-
-            @pl.when(peer != me)
-            def _():
-                to_peer(terms, terms_got, terms_sems, peer, me).start()
-
-        return carry
-
-    lax.fori_loop(0, SEQ_BLOCKS // 2, term_step, 0)
 
     arrived(grad, grad_got, grad_sems)
     take_blocks(grad_got, grid)
@@ -390,13 +436,23 @@
     taps_store.start()
     skip_gradient(grad_got, gated_got, skip_out)
 
-    weight_res[...] = terms[me].astype(jnp.float32)
-
-    def sum_step(i, carry):
-        peer = (me + SEQ_BLOCKS - i) % SEQ_BLOCKS
-        to_peer(terms, terms_got, terms_sems, peer, peer).wait_recv()
-        weight_res[...] += terms_got[peer].astype(jnp.float32)
-        return carry
+    def summed(half, stage, held, got, j, columns):
+        own = z if half == stage else y
+        total = held[half, own, term_rows(j), columns].astype(jnp.float32)
+        for k in (1, 2, 3):
+            total += got[half, (own + k) % 4, term_rows(j), columns].astype(jnp.float32)
+        return total
+
+    for j in range(TERM_CHUNKS):
+        for half in range(2):
+            for k in (1, 3, 2):
+                from_peer(half, 0, terms, terms_got, terms_sems, j, k).wait_recv()
+            for place in range(4):
+                columns = pl.ds(place * 256, 256)
+                total = summed(half, 0, terms, terms_got, j, columns)
+                second_terms[half, place, term_rows(j)] = total.astype(jnp.bfloat16)
+            for k in (2, 1, 3):
+                one_of(half, 1, second_terms, second_got, second_sems, j, k).start()
 
     arrived(back, back_got, back_sems)
 
@@ -410,7 +466,22 @@
     key_store.start()
     value_store = pltpu.make_async_copy(value_res, value_out, store_sem.at[3])
     value_store.start()
-    lax.fori_loop(1, SEQ_BLOCKS, sum_step, 0)
+    mine = pl.ds(pl.multiple_of(x * LANES, LANES), LANES)
+    others = pl.ds(pl.multiple_of((1 - x) * LANES, LANES), LANES)
+    for j in range(TERM_CHUNKS):
+        for half in range(2):
+            for k in (1, 3, 2):
+                from_peer(half, 1, second_terms, second_got, second_sems, j, k).wait_recv()
+            third[half, term_rows(j)] = summed(half, 1, second_terms, second_got, j, others).astype(jnp.bfloat16)
+            side_of(half, j).start()
+            weight_res[pl.ds(half * 256 + j * TERM_ROWS, TERM_ROWS), :] = summed(
+                half, 1, second_terms, second_got, j, mine
+            )
+    for j in range(TERM_CHUNKS):
+        for half in range(2):
+            side_of(half, j).wait_recv()
+            rows = pl.ds(half * 256 + j * TERM_ROWS, TERM_ROWS)
+            weight_res[rows, :] += third_got[half, term_rows(j)].astype(jnp.float32)
     weight_store = pltpu.make_async_copy(weight_res, weight_out, store_sem.at[4])
     weight_store.start()
 
@@ -418,12 +489,30 @@
     sent(conv, conv_got, conv_sems)
     sent(grad, grad_got, grad_sems)
     sent(back, back_got, back_sems)
-    sent(terms, terms_got, terms_sems)
+    for j in range(TERM_CHUNKS):
+        for half in range(2):
+            for k in (1, 2, 3):
+                one_of(half, 0, terms, terms_got, terms_sems, j, k).wait_send()
+                one_of(half, 1, second_terms, second_got, second_sems, j, k).wait_send()
+            side_of(half, j).wait_send()
     near.wait_send()
     for j in range(COT_CHUNKS):
         far(j).wait_send()
         relay(j).wait_send()
     for copy in (query_store, taps_store, key_store, value_store, weight_store):
+        copy.wait()
+
+
+def hand_over(*refs):
+    sources, targets, held, sems = refs[:6], refs[6:12], refs[12:18], refs[18]
+    loads = [pltpu.make_async_copy(a, b, sems.at[0, i]) for i, (a, b) in enumerate(zip(sources, held))]
+    stores = [pltpu.make_async_copy(a, b, sems.at[1, i]) for i, (a, b) in enumerate(zip(held, targets))]
+    for copy in loads:
+        copy.start()
+    for load, store in zip(loads, stores):
+        load.wait()
+        store.start()
+    for copy in stores:
         copy.wait()
 
 
@@ -435,29 +524,32 @@
     in_vmem = pl.BlockSpec(memory_space=pltpu.VMEM)
     block_buffer = pltpu.VMEM(blocks, bf16)
     spec_buffer = pltpu.VMEM((CHANS * ROWS, 2 * COLS), f32)
-    terms_buffer = pltpu.VMEM((SEQ_BLOCKS, 512, LANES), bf16)
-    peer_sems = pltpu.SemaphoreType.DMA((2, SEQ_BLOCKS))
+    terms_buffer = pltpu.VMEM((2, 4, 256, 1024), bf16)
+    second_buffer = pltpu.VMEM((2, 4, 256, 256), bf16)
+    third_buffer = pltpu.VMEM((2, 256, LANES), bf16)
     dma = pltpu.SemaphoreType.DMA
-    grad_query, grad_key, grad_value, grad_filter, grad_skip, grad_weight = pl.pallas_call(
+    shapes = (
+        jax.ShapeDtypeStruct(blocks, bf16),
+        jax.ShapeDtypeStruct(blocks, bf16),
+        jax.ShapeDtypeStruct(blocks, bf16),
+        jax.ShapeDtypeStruct(filter_taps.shape, f32),
+        jax.ShapeDtypeStruct((1, CHANS), f32),
+        jax.ShapeDtypeStruct((512, LANES), f32),
+    )
+    results = pl.pallas_call(
         kernel,
-        out_shape=(
-            jax.ShapeDtypeStruct(blocks, bf16),
-            jax.ShapeDtypeStruct(blocks, bf16),
-            jax.ShapeDtypeStruct(blocks, bf16),
-            jax.ShapeDtypeStruct(filter_taps.shape, f32),
-            jax.ShapeDtypeStruct((1, CHANS), f32),
-            jax.ShapeDtypeStruct((512, LANES), f32),
-        ),
+        out_shape=shapes,
         in_specs=[in_hbm] * 4 + [in_vmem] + [in_hbm] * 6,
         out_specs=[in_hbm] * 4 + [in_vmem, in_hbm],
         scratch_shapes=[
             block_buffer, block_buffer, block_buffer,
             pltpu.VMEM(filter_taps.shape, f32),
             pltpu.VMEM(out_weight.shape, bf16),
-            *[pltpu.VMEM(t.shape, t.dtype) for t in constants],
+            *[pltpu.VMEM(t.shape, f32) for t in constants],
+            *[pltpu.VMEM(t.shape, bf16) for t in (constants[0], constants[1], constants[3])],
             pltpu.VMEM((4, 512, 1024), bf16),
             *[block_buffer] * 8,
-            terms_buffer, terms_buffer,
+            terms_buffer, terms_buffer, second_buffer, second_buffer, third_buffer, third_buffer,
             pltpu.VMEM((512, 512), f32),
             pltpu.VMEM((512, 512), bf16),
             pltpu.VMEM((2, CHANS * ROWS, LANES), f32),
@@ -467,7 +559,8 @@
             pltpu.VMEM(filter_taps.shape, f32),
             pltpu.VMEM((512, LANES), f32),
             dma((10,)), dma((5,)),
-            *[peer_sems] * 5,
+            *[dma((2,))] * 4,
+            dma((2, 2, TERM_CHUNKS, 3)), dma((2, 2, TERM_CHUNKS, 3)), dma((2, 2, TERM_CHUNKS)),
             dma((2,)), dma((2, COT_CHUNKS)), dma((2, COT_CHUNKS)),
         ],
         compiler_params=pltpu.CompilerParams(
@@ -477,6 +570,14 @@
         query_gate.reshape(blocks), key_branch.reshape(blocks), value_branch.reshape(blocks), filter_taps,
         skip_gain[None, :], out_weight, out_grad, *constants,
     )
+    grad_query, grad_key, grad_value, grad_filter, grad_skip, grad_weight = pl.pallas_call(
+        hand_over,
+        out_shape=shapes,
+        in_specs=[in_hbm] * 6,
+        out_specs=[in_hbm] * 6,
+        scratch_shapes=[*[pltpu.VMEM(t.shape, t.dtype) for t in shapes], dma((2, 6))],
+        compiler_params=pltpu.CompilerParams(vmem_limit_bytes=56 * 1024 * 1024),
+    )(*results)
     shape = query_gate.shape
     return (
         grad_query.reshape(shape), grad_key.reshape(shape), grad_value.reshape(shape),

time: 146 us -> 99.5 us (0.68)
  Pallas kernels: 136 us -> 98.7 us
  local copies, waits for them, and re-layouts: 9.13 us -> 0 us
    pallas_call x1 -> x2, Pallas kernels: 136 us -> 98.7 us  [the longest x1 95.8 us: body(): pl.pallas_call(kernel, out_shape=shapes, in_specs=[in_hbm] * 4 + [in_vmem...]
    unnamed x10 -> x0, local copies, waits for them, and re-layouts: 9.13 us -> none
where the time goes in v2:
time: 99.5 us; the launch traced here: 99.3 us
  Pallas kernels  98.7 us (99%)
    pallas_call x1, Pallas kernels, body(): pl.pallas_call(kernel, out_shape=shapes, in_specs=[in_hbm] * 4 + [in_vmem...  95.8 us
    pallas_call x1, Pallas kernels, body(): pl.pallas_call(hand_over, out_shape=shapes, in_specs=[in_hbm] * 6, out_sp...  2.86 us

profile of v2, /device:TPU:1, one launch (start us, length us, event | category | flops | bytes accessed | tf_op | source)
XLA Modules:
  0.0 99.3 jit_solution(13665926526122072980)
XLA Ops:
  0.6 95.8 %shard_map.154 = (bf16[32,16,512]{2,1,0:T(8,128)(2,1)}, bf16[32,16,512]{2,1,0:T(8,128)(2,1)}, bf16[32,16,512]{2,1,0:T(8,128)(2,1)}, f32[16,16384]{1,0:T(8,128)}, f32[1,16]{1,0:T(1,128)}, /*index=5*/f32[512,128]{1,0:T(8,128)}) custom-call(bf16[32,16,512]{2,1,0:T(8,128)(2,1)} %bitcast.8, bf16[32,16,512]{2,1,0:T(8,128)(2,1)} %bitcast.9, ...), custom_call_target="tpu_custom_call" | custom-call | tf_op jit(solution)/shard_map/pallas_call | solution.py:539
  96.4 2.9 %shard_map.155 = (bf16[32,16,512]{2,1,0:T(8,128)(2,1)}, bf16[32,16,512]{2,1,0:T(8,128)(2,1)}, bf16[32,16,512]{2,1,0:T(8,128)(2,1)}, f32[16,16384]{1,0:T(8,128)}, f32[1,16]{1,0:T(1,128)}, /*index=5*/f32[512,128]{1,0:T(8,128)}) custom-call(bf16[32,16,512]{2,1,0:T(8,128)(2,1)} %get-tuple-element.18.refs_0_, bf16[32,16,512]{2,1,0:T(8,128)(2,1)} %get-tuple-element.19.refs_1_, ...), custom_call_target="tpu_custom_call" | custom-call | tf_op jit(solution)/shard_map/pallas_call | solution.py:573

commit v3 on v2

--- a/solution.py
+++ b/solution.py
@@ -12,10 +12,9 @@
 LANES = 128
 CHANS = 16
 SEQ_BLOCKS = 32
-COT_CHUNKS = 4
-COT_ROWS = 128
 TERM_CHUNKS = 2
-TERM_ROWS = 256 // TERM_CHUNKS
+Z_FIRST = 192
+TERM_SPANS = ((0, Z_FIRST), (Z_FIRST, 512))
 
 
 def bf16_pair(values):
@@ -62,12 +61,7 @@
 
 
 def second_stage(mixed, second_ref, out):
-    def step(i, carry):
-        rows = pl.ds(pl.multiple_of(i * 256, 256), 256)
-        out[rows, :] = dot(mixed[rows, :], second_ref[...])
-        return carry
-
-    lax.fori_loop(0, CHANS * ROWS // 256, step, 0)
+    out[...] = dot(mixed[...], second_ref[...])
 
 
 def spectrum_of(grid, first_ref, turn_ref, second_ref, mixed, out, wide):
@@ -87,7 +81,7 @@
         mixed[rows, COLS:] = im.astype(jnp.bfloat16)
         return carry
 
-    lax.fori_loop(0, CHANS, step, 0, unroll=4)
+    lax.fori_loop(0, CHANS, step, 0, unroll=16)
     second_stage(mixed, second_ref, out)
 
 
@@ -121,7 +115,7 @@
             grid[half, pl.ds(c, ROWS, stride=CHANS), :] = signal[:, half * LANES : (half + 1) * LANES]
         return carry
 
-    lax.fori_loop(0, CHANS, step, 0, unroll=4)
+    lax.fori_loop(0, CHANS, step, 0, unroll=16)
 
 
 def give_blocks(grid, blocks_ref):
@@ -180,11 +174,16 @@
     query_in, key_in, value_in, taps_in, skip_ref, weight_in, cot_in, first_in, last_in, turn_in, second_in,
     query_out, key_out, value_out, taps_out, skip_out, weight_out,
     query, key, value, taps, weight, first_wide, last_wide, turn, second_wide, first, last, second,
-    cot, gated, gated_got, conv, conv_got, grad, grad_got, back, back_got, terms, terms_got,
-    second_terms, second_got, third, third_got, grad_mixed, gate_mixed,
+    cot, gated, gated_got, conv, conv_got, grad, grad_got, back, back_got,
+    terms_z, terms_y, terms_got_z, terms_got_y, second_z, second_y, second_got_z, second_got_y,
+    third_z, third_y, third_got_z, third_got_y, grad_mixed, gate_mixed,
     grid, mixed, spec, taps_spec, gated_spec, grad_spec, query_res, key_res, value_res, taps_res, weight_res,
-    load_sem, store_sem, gated_sems, conv_sems, grad_sems, back_sems, terms_sems, second_sems, third_sems, near_sems, far_sems, relay_sems,
+    load_sem, store_sem, gated_sems, conv_sems, grad_sems, back_sems, terms_sems, second_sems, third_sems,
+    near_sems, far_sems, relay_sems,
 ):
+    terms, terms_got = (terms_z, terms_y), (terms_got_z, terms_got_y)
+    second_terms, second_got = (second_z, second_y), (second_got_z, second_got_y)
+    third, third_got = (third_z, third_y), (third_got_z, third_got_y)
     me = lax.axis_index("ctx")
     part = lax.axis_index("tp")
     sibling = part + 1 - 2 * (part % 2)
@@ -269,31 +268,32 @@
     )
     near.start()
 
-    def chunk_rows(j):
-        return pl.ds(j * COT_ROWS, COT_ROWS)
-
-    def far(j):
-        return pltpu.make_async_remote_copy(
-            src_ref=cot_in.at[chunk_rows(j)],
-            dst_ref=cot.at[part, chunk_rows(j)],
-            send_sem=far_sems.at[0, j],
-            recv_sem=far_sems.at[1, j],
-            device_id={"tp": across},
-            device_id_type=pl.DeviceIdType.MESH,
-        )
-
-    def relay(j):
-        return pltpu.make_async_remote_copy(
-            src_ref=cot.at[across, chunk_rows(j)],
-            dst_ref=cot.at[across, chunk_rows(j)],
-            send_sem=relay_sems.at[0, j],
-            recv_sem=relay_sems.at[1, j],
-            device_id={"tp": sibling},
-            device_id_type=pl.DeviceIdType.MESH,
-        )
-
-    for j in range(COT_CHUNKS):
-        far(j).start()
+    def cot_block(p, parity, half, q):
+        columns = pl.ds(q * 256 + parity * LANES, LANES)
+        return cot.at[p, pl.ds(half * 256, 256), columns]
+
+    def chunk_bytes(p, parity, half, sems, device):
+        window = cot.at[p, pl.ds(half * 256, 256), pl.ds(0, 512)]
+        return to_device(window, window, sems.at[0, parity, half], sems.at[1, parity, half], device)
+
+    def far_start(parity, half):
+        for q in range(4):
+            columns = pl.ds(q * 256 + parity * LANES, LANES)
+            to_device(
+                cot_in.at[pl.ds(half * 256, 256), columns], cot_block(part, parity, half, q),
+                far_sems.at[0, parity, half], far_sems.at[1, parity, half], {"tp": across},
+            ).start()
+
+    def relay_start(parity, half):
+        chunk_bytes(across, parity, half, far_sems, {"tp": across}).wait_recv()
+        for q in range(4):
+            block = cot_block(across, parity, half, q)
+            to_device(
+                block, block, relay_sems.at[0, parity, half], relay_sems.at[1, parity, half], {"tp": sibling}
+            ).start()
+
+    def relay_arrived(parity, half):
+        chunk_bytes(diagonal, parity, half, relay_sems, {"tp": sibling}).wait_recv()
 
     taps_load.wait()
     first_load.wait()
@@ -304,10 +304,10 @@
     taps_to_grid(taps, skip_ref, grid)
     spectrum_of(grid, first, turn, second, mixed, taps_spec, True)
 
-    def mix_features(p, fresh):
-        def step(i, carry):
-            rows = pl.ds(pl.multiple_of(i * 256, 256), 256)
-            columns = pl.ds(pl.multiple_of(p * 1024, 1024), 1024)
+    def mix_features(p, fresh, halves=(0, 1)):
+        columns = pl.ds(pl.multiple_of(p * 1024, 1024), 1024)
+        for half in halves:
+            rows = pl.ds(half * 256, 256)
             term = lax.dot_general(
                 weight[:, columns], cot[p, rows, :], (((1,), (1,)), ((), ())),
                 preferred_element_type=jnp.float32,
@@ -316,9 +316,17 @@
                 grad_mixed[:, rows] = term
             else:
                 grad_mixed[:, rows] += term
-            return carry
-
-        lax.fori_loop(0, 2, step, 0)
+
+    def mix_chunk(p, parity, half):
+        rows = pl.ds(half * 256, 256)
+        left = [
+            weight[:, pl.ds(pl.multiple_of(p * 1024 + q * 256 + parity * LANES, LANES), LANES)] for q in range(4)
+        ]
+        right = [cot[p, rows, pl.ds(q * 256 + parity * LANES, LANES)] for q in range(4)]
+        grad_mixed[:, rows] += lax.dot_general(
+            jnp.concatenate(left, axis=1), jnp.concatenate(right, axis=1), (((1,), (1,)), ((), ())),
+            preferred_element_type=jnp.float32,
+        )
 
     cot_load.wait()
     weight_load.wait()
@@ -328,6 +336,7 @@
     query_load.wait()
 
     arrived(gated, gated_got, gated_sems)
+    far_start(0, 0)
     take_blocks(gated_got, grid)
     spectrum_of(grid, first, turn, second, mixed, gated_spec, False)
     product_to(mixed, taps_spec, gated_spec, False)
@@ -335,9 +344,49 @@
     give_blocks(grid, conv)
     exchange(conv, conv_got, conv_sems)
 
+    def half_exchange(half, source, target, peer):
+        columns = pl.ds(half * 256, 256)
+        return to_device(
+            source.at[peer, :, columns], target.at[me, :, columns], grad_sems.at[0, half], grad_sems.at[1, half],
+            {"ctx": peer},
+        )
+
+    def whole_half(half):
+        blocks, columns = pl.ds(0, SEQ_BLOCKS - 1), pl.ds(half * 256, 256)
+        return to_device(
+            grad.at[blocks, :, columns], grad_got.at[blocks, :, columns], grad_sems.at[0, half],
+            grad_sems.at[1, half], {"tp": across},
+        )
+
+    def take_chunk(parity, half):
+        relay_start(parity, half)
+        mix_chunk(across, parity, half)
+        relay_arrived(parity, half)
+        mix_chunk(diagonal, parity, half)
+
+    def send_gradient(half):
+        columns = pl.ds(half * 256, 256)
+
+        def cotangent(s):
+            grad[s, :, columns] = (
+                grad_mixed[block_rows(s), columns] * query[s, :, columns].astype(jnp.float32)
+            ).astype(jnp.bfloat16)
+
+        for_blocks(cotangent)
+
+        def step(i, carry):
+            half_exchange(half, grad, grad_got, (me + i) % SEQ_BLOCKS).start()
+            return carry
+
+        lax.fori_loop(1, SEQ_BLOCKS, step, 0)
+        grad_got[me, :, columns] = grad[me, :, columns]
+
     near.wait_recv()
     mix_features(sibling, False)
     arrived(conv, conv_got, conv_sems)
+    far_start(0, 1)
+    far_start(1, 0)
+    far_start(1, 1)
 
     def gate_output(s):
         gate_mixed[block_rows(s), :] = (
@@ -345,75 +394,118 @@
         ).astype(jnp.bfloat16)
 
     for_blocks(gate_output)
-    for j in range(COT_CHUNKS):
-        far(j).wait_recv()
-        relay(j).start()
-    mix_features(across, False)
-    for j in range(COT_CHUNKS):
-        relay(j).wait_recv()
-    mix_features(diagonal, False)
-
-    def cotangent(s):
-        grad[s] = (grad_mixed[block_rows(s), :] * query[s].astype(jnp.float32)).astype(jnp.bfloat16)
-
-    for_blocks(cotangent)
-    exchange(grad, grad_got, grad_sems)
 
     z, y, x = me // 8, me // 2 % 4, me % 2
-
-    def z_peer(k):
-        return (z + k) % 4
-
-    def y_peer(k):
-        return (y + k) % 4
-
-    def peer_of(half, stage, k):
-        if half == stage:
-            return z_peer(k), {"ctx": z_peer(k) * 8 + y * 2 + x}, z
-        return y_peer(k), {"ctx": z * 8 + y_peer(k) * 2 + x}, y
-
-    def term_rows(j):
-        return pl.ds(pl.multiple_of(j * TERM_ROWS, TERM_ROWS), TERM_ROWS)
-
-    def one_of(half, stage, source, target, sems, j, k):
-        place, device, own = peer_of(half, stage, k)
+    chip = part // 2
+
+    def peer_of(order, stage, k):
+        if order == stage:
+            return (z + k) % 4, {"ctx": (z + k) % 4 * 8 + y * 2 + x}, z
+        return (y + k) % 4, {"ctx": z * 8 + (y + k) % 4 * 2 + x}, y
+
+    def chunk_span(order, j):
+        start, stop = TERM_SPANS[order]
+        rows = (stop - start) // TERM_CHUNKS
+        return pl.ds(j * rows, rows)
+
+    def first_columns(order, piece):
+        if order == 0:
+            return pl.ds(0, 1024) if piece == 0 else pl.ds((piece - 1) * 512, 512)
+        if piece == 0:
+            return pl.ds(pl.multiple_of(chip * 512, 512), 512)
+        return pl.ds(pl.multiple_of((1 - chip) * 512 + (piece - 1) * 256, 256), 256)
+
+    def first_send(order, piece, j, k):
+        place, device, own = peer_of(order, 0, k)
+        rows, columns = chunk_span(order, j), first_columns(order, piece)
         return to_device(
-            source.at[half, place, term_rows(j)], target.at[half, own, term_rows(j)],
-            sems.at[0, half, j, k - 1], sems.at[1, half, j, k - 1], device,
-        )
-
-    def side_of(half, j):
+            terms[order].at[place, rows, columns], terms_got[order].at[own, rows, columns],
+            terms_sems.at[0, order, j, k - 1], terms_sems.at[1, order, j, k - 1], device,
+        )
+
+    def first_whole(order, j, k):
+        place, device, own = peer_of(order, 0, 4 - k)
+        rows = chunk_span(order, j)
         return to_device(
-            third.at[half, term_rows(j)], third_got.at[half, term_rows(j)],
-            third_sems.at[0, half, j], third_sems.at[1, half, j], {"ctx": me + 1 - 2 * x},
-        )
-
-    def from_peer(half, stage, source, target, sems, j, k):
-        place, device, own = peer_of(half, stage, 4 - k)
+            terms[order].at[place, rows], terms_got[order].at[place, rows],
+            terms_sems.at[0, order, j, k - 1], terms_sems.at[1, order, j, k - 1], device,
+        )
+
+    def second_send(order, j, k):
+        place, device, own = peer_of(order, 1, k)
+        rows = chunk_span(order, j)
         return to_device(
-            source.at[half, place, term_rows(j)], target.at[half, place, term_rows(j)],
-            sems.at[0, half, j, k - 1], sems.at[1, half, j, k - 1], device,
-        )
-
-    def term_chunk(j):
+            second_terms[order].at[place, rows], second_got[order].at[own, rows],
+            second_sems.at[0, order, j, k - 1], second_sems.at[1, order, j, k - 1], device,
+        )
+
+    def second_arrival(order, j, k):
+        place, device, own = peer_of(order, 1, 4 - k)
+        rows = chunk_span(order, j)
+        return to_device(
+            second_terms[order].at[place, rows], second_got[order].at[place, rows],
+            second_sems.at[0, order, j, k - 1], second_sems.at[1, order, j, k - 1], device,
+        )
+
+    def side_of(order, j):
+        rows = chunk_span(order, j)
+        return to_device(
+            third[order].at[rows], third_got[order].at[rows],
+            third_sems.at[0, order, j], third_sems.at[1, order, j], {"ctx": me + 1 - 2 * x},
+        )
+
+    def keep_term(p, q, parity, term):
+        columns = pl.ds(pl.multiple_of(parity * 512 + q * LANES, LANES), LANES)
+        terms[0][p, :, columns] = term[:Z_FIRST]
+        columns = pl.ds(pl.multiple_of(p // 2 * 512 + parity * 256 + p % 2 * LANES, LANES), LANES)
+        terms[1][q, :, columns] = term[Z_FIRST:]
+
+    def make_terms():
         def step(i, carry):
-            p, q = i // 4, i % 4
+            p, q = chip * 2 + i // 4, i % 4
             columns = pl.ds(pl.multiple_of(q * 256, 256), 256)
-            targets = pl.ds(pl.multiple_of(p * 256, 256), 256)
-            lower = pl.ds(pl.multiple_of(256 + j * TERM_ROWS, TERM_ROWS), TERM_ROWS)
-            left = jnp.concatenate([gate_mixed[term_rows(j), :], gate_mixed[lower, :]], axis=0)
-            term = dot(left, cot[p, :, columns]).astype(jnp.bfloat16)
-            terms[0, p, term_rows(j), columns] = term[:TERM_ROWS]
-            terms[1, q, term_rows(j), targets] = term[TERM_ROWS:]
+            term = dot(gate_mixed[...], cot[p, :, columns]).astype(jnp.bfloat16)
+            for parity in range(2):
+                keep_term(p, q, parity, term[:, parity * LANES : (parity + 1) * LANES])
             return carry
 
-        lax.fori_loop(0, 16, step, 0)
-        for k in (2, 1, 3):
-            for half in range(2):
-                one_of(half, 0, terms, terms_got, terms_sems, j, k).start()
-
-    for j in range(TERM_CHUNKS):
-        term_chunk(j)
+        lax.fori_loop(0, 8, step, 0)
+
+    def make_late_terms(parity):
+        def step(i, carry):
+            p, q = (1 - chip) * 2 + i // 2, i % 2 * 2
+            right = [
+                cot[p, :, pl.ds(pl.multiple_of((q + n) * 256 + parity * LANES, LANES), LANES)] for n in range(2)
+            ]
+            term = dot(gate_mixed[...], jnp.concatenate(right, axis=1)).astype(jnp.bfloat16)
+            for n in range(2):
+                keep_term(p, q + n, parity, term[:, n * LANES : (n + 1) * LANES])
+            return carry
+
+        lax.fori_loop(0, 4, step, 0)
+
+    def send_terms(piece):
+        for j in range(TERM_CHUNKS):
+            for k in (2, 1, 3):
+                first_send(1, piece, j, k).start()
+                here = (z + k) % 4 // 2 == chip
+
+                @pl.when(here if piece == 0 else jnp.logical_not(here))
+                def _():
+                    first_send(0, piece, j, k).start()
+
+    make_terms()
+    send_terms(0)
+    take_chunk(0, 0)
+    take_chunk(0, 1)
+    make_late_terms(0)
+    send_terms(1)
+    take_chunk(1, 0)
+    send_gradient(0)
+    take_chunk(1, 1)
+    send_gradient(1)
+    make_late_terms(1)
+    send_terms(2)
 
     def query_gradient(s):
         query_res[s] = (grad_mixed[block_rows(s), :] * conv_got[s].astype(jnp.float32)).astype(jnp.bfloat16)
@@ -422,7 +514,8 @@
     query_store = pltpu.make_async_copy(query_res, query_out, store_sem.at[0])
     query_store.start()
 
-    arrived(grad, grad_got, grad_sems)
+    for half in range(2):
+        whole_half(half).wait_recv()
     take_blocks(grad_got, grid)
     spectrum_of(grid, first, turn, second, mixed, grad_spec, False)
     product_to(mixed, taps_spec, grad_spec, True)
@@ -436,23 +529,29 @@
     taps_store.start()
     skip_gradient(grad_got, gated_got, skip_out)
 
-    def summed(half, stage, held, got, j, columns):
-        own = z if half == stage else y
-        total = held[half, own, term_rows(j), columns].astype(jnp.float32)
+    def summed(order, stage, held, got, j, columns):
+        own = z if order == stage else y
+        rows = chunk_span(order, j)
+        total = held[order][own, rows, columns].astype(jnp.float32)
         for k in (1, 2, 3):
-            total += got[half, (own + k) % 4, term_rows(j), columns].astype(jnp.float32)
+            total += got[order][(own + k) % 4, rows, columns].astype(jnp.float32)
         return total
 
     for j in range(TERM_CHUNKS):
-        for half in range(2):
+        for order in range(2):
             for k in (1, 3, 2):
-                from_peer(half, 0, terms, terms_got, terms_sems, j, k).wait_recv()
+                first_whole(order, j, k).wait_recv()
             for place in range(4):
-                columns = pl.ds(place * 256, 256)
-                total = summed(half, 0, terms, terms_got, j, columns)
-                second_terms[half, place, term_rows(j)] = total.astype(jnp.bfloat16)
+                for parity in range(2):
+                    if order == 0:
+                        start = parity * 512 + place * LANES
+                    else:
+                        start = place // 2 * 512 + parity * 256 + place % 2 * LANES
+                    total = summed(order, 0, terms, terms_got, j, pl.ds(start, LANES))
+                    columns = pl.ds(parity * LANES, LANES)
+                    second_terms[order][place, chunk_span(order, j), columns] = total.astype(jnp.bfloat16)
             for k in (2, 1, 3):
-                one_of(half, 1, second_terms, second_got, second_sems, j, k).start()
+                second_send(order, j, k).start()
 
     arrived(back, back_got, back_sems)
 
@@ -468,37 +567,43 @@
     value_store.start()
     mine = pl.ds(pl.multiple_of(x * LANES, LANES), LANES)
     others = pl.ds(pl.multiple_of((1 - x) * LANES, LANES), LANES)
+
+    def result_rows(order, j):
+        start, stop = TERM_SPANS[order]
+        rows = (stop - start) // TERM_CHUNKS
+        return pl.ds(start + j * rows, rows)
+
     for j in range(TERM_CHUNKS):
-        for half in range(2):
+        for order in range(2):
             for k in (1, 3, 2):
-                from_peer(half, 1, second_terms, second_got, second_sems, j, k).wait_recv()
-            third[half, term_rows(j)] = summed(half, 1, second_terms, second_got, j, others).astype(jnp.bfloat16)
-            side_of(half, j).start()
-            weight_res[pl.ds(half * 256 + j * TERM_ROWS, TERM_ROWS), :] = summed(
-                half, 1, second_terms, second_got, j, mine
-            )
+                second_arrival(order, j, k).wait_recv()
+            total = summed(order, 1, second_terms, second_got, j, others)
+            third[order][chunk_span(order, j)] = total.astype(jnp.bfloat16)
+            side_of(order, j).start()
+            weight_res[result_rows(order, j), :] = summed(order, 1, second_terms, second_got, j, mine)
     for j in range(TERM_CHUNKS):
-        for half in range(2):
-            side_of(half, j).wait_recv()
-            rows = pl.ds(half * 256 + j * TERM_ROWS, TERM_ROWS)
-            weight_res[rows, :] += third_got[half, term_rows(j)].astype(jnp.float32)
+        for order in range(2):
+            side_of(order, j).wait_recv()
+            weight_res[result_rows(order, j), :] += third_got[order][chunk_span(order, j)].astype(jnp.float32)
     weight_store = pltpu.make_async_copy(weight_res, weight_out, store_sem.at[4])
     weight_store.start()
 
     sent(gated, gated_got, gated_sems)
     sent(conv, conv_got, conv_sems)
-    sent(grad, grad_got, grad_sems)
+    for half in range(2):
+        whole_half(half).wait_send()
     sent(back, back_got, back_sems)
     for j in range(TERM_CHUNKS):
+        for order in range(2):
+            for k in (1, 2, 3):
+                first_whole(order, j, k).wait_send()
+                second_send(order, j, k).wait_send()
+            side_of(order, j).wait_send()
+    near.wait_send()
+    for parity in range(2):
         for half in range(2):
-            for k in (1, 2, 3):
-                one_of(half, 0, terms, terms_got, terms_sems, j, k).wait_send()
-                one_of(half, 1, second_terms, second_got, second_sems, j, k).wait_send()
-            side_of(half, j).wait_send()
-    near.wait_send()
-    for j in range(COT_CHUNKS):
-        far(j).wait_send()
-        relay(j).wait_send()
+            chunk_bytes(part, parity, half, far_sems, {"tp": across}).wait_send()
+            chunk_bytes(across, parity, half, relay_sems, {"tp": sibling}).wait_send()
     for copy in (query_store, taps_store, key_store, value_store, weight_store):
         copy.wait()
 
@@ -524,9 +629,10 @@
     in_vmem = pl.BlockSpec(memory_space=pltpu.VMEM)
     block_buffer = pltpu.VMEM(blocks, bf16)
     spec_buffer = pltpu.VMEM((CHANS * ROWS, 2 * COLS), f32)
-    terms_buffer = pltpu.VMEM((2, 4, 256, 1024), bf16)
-    second_buffer = pltpu.VMEM((2, 4, 256, 256), bf16)
-    third_buffer = pltpu.VMEM((2, 256, LANES), bf16)
+    spans = [stop - start for start, stop in TERM_SPANS]
+    terms_buffers = [pltpu.VMEM((4, rows, 1024), bf16) for rows in spans]
+    second_buffers = [pltpu.VMEM((4, rows, 256), bf16) for rows in spans]
+    third_buffers = [pltpu.VMEM((rows, LANES), bf16) for rows in spans]
     dma = pltpu.SemaphoreType.DMA
     shapes = (
         jax.ShapeDtypeStruct(blocks, bf16),
@@ -549,7 +655,7 @@
             *[pltpu.VMEM(t.shape, bf16) for t in (constants[0], constants[1], constants[3])],
             pltpu.VMEM((4, 512, 1024), bf16),
             *[block_buffer] * 8,
-            terms_buffer, terms_buffer, second_buffer, second_buffer, third_buffer, third_buffer,
+            *terms_buffers * 2, *second_buffers * 2, *third_buffers * 2,
             pltpu.VMEM((512, 512), f32),
             pltpu.VMEM((512, 512), bf16),
             pltpu.VMEM((2, CHANS * ROWS, LANES), f32),
@@ -559,9 +665,9 @@
             pltpu.VMEM(filter_taps.shape, f32),
             pltpu.VMEM((512, LANES), f32),
             dma((10,)), dma((5,)),
-            *[dma((2,))] * 4,
+            dma((2,)), dma((2,)), dma((2, 2)), dma((2,)),
             dma((2, 2, TERM_CHUNKS, 3)), dma((2, 2, TERM_CHUNKS, 3)), dma((2, 2, TERM_CHUNKS)),
-            dma((2,)), dma((2, COT_CHUNKS)), dma((2, COT_CHUNKS)),
+            dma((2,)), dma((2, 2, 2)), dma((2, 2, 2)),
         ],
         compiler_params=pltpu.CompilerParams(
             collective_id=0, has_side_effects=True, vmem_limit_bytes=56 * 1024 * 1024

time: 99.5 us -> 91.1 us (0.916)
  Pallas kernels: 98.7 us -> 90.3 us
    pallas_call x1, Pallas kernels: 95.8 us -> 87.4 us  [body(): pl.pallas_call(kernel, out_shape=shapes, in_specs=[in_hbm] * 4 + [in_vmem...]
where the time goes in v3:
time: 91.1 us; the launch traced here: 90.9 us
  Pallas kernels  90.3 us (99%)
    pallas_call x1, Pallas kernels, body(): pl.pallas_call(kernel, out_shape=shapes, in_specs=[in_hbm] * 4 + [in_vmem...  87.4 us
    pallas_call x1, Pallas kernels, body(): pl.pallas_call(hand_over, out_shape=shapes, in_specs=[in_hbm] * 6, out_sp...  2.86 us

profile of v3, /device:TPU:1, one launch (start us, length us, event | category | flops | bytes accessed | tf_op | source)
XLA Modules:
  0.0 90.9 jit_solution(13986116612420963941)
XLA Ops:
  0.6 87.4 %shard_map.154 = (bf16[32,16,512]{2,1,0:T(8,128)(2,1)}, bf16[32,16,512]{2,1,0:T(8,128)(2,1)}, bf16[32,16,512]{2,1,0:T(8,128)(2,1)}, f32[16,16384]{1,0:T(8,128)}, f32[1,16]{1,0:T(1,128)}, /*index=5*/f32[512,128]{1,0:T(8,128)}) custom-call(bf16[32,16,512]{2,1,0:T(8,128)(2,1)} %bitcast.8, bf16[32,16,512]{2,1,0:T(8,128)(2,1)} %bitcast.9, ...), custom_call_target="tpu_custom_call" | custom-call | tf_op jit(solution)/shard_map/pallas_call | solution.py:645
  88.1 2.9 %shard_map.155 = (bf16[32,16,512]{2,1,0:T(8,128)(2,1)}, bf16[32,16,512]{2,1,0:T(8,128)(2,1)}, bf16[32,16,512]{2,1,0:T(8,128)(2,1)}, f32[16,16384]{1,0:T(8,128)}, f32[1,16]{1,0:T(1,128)}, /*index=5*/f32[512,128]{1,0:T(8,128)}) custom-call(bf16[32,16,512]{2,1,0:T(8,128)(2,1)} %get-tuple-element.18.refs_0_, bf16[32,16,512]{2,1,0:T(8,128)(2,1)} %get-tuple-element.19.refs_1_, ...), custom_call_target="tpu_custom_call" | custom-call | tf_op jit(solution)/shard_map/pallas_call | solution.py:679

commit v4 on v3

--- a/solution.py
+++ b/solution.py
@@ -12,7 +12,6 @@
 LANES = 128
 CHANS = 16
 SEQ_BLOCKS = 32
-TERM_CHUNKS = 2
 Z_FIRST = 192
 TERM_SPANS = ((0, Z_FIRST), (Z_FIRST, 512))
 
@@ -172,13 +171,13 @@
 
 def kernel(
     query_in, key_in, value_in, taps_in, skip_ref, weight_in, cot_in, first_in, last_in, turn_in, second_in,
-    query_out, key_out, value_out, taps_out, skip_out, weight_out,
+    query_res, key_res, value_res, taps_res, skip_out, weight_res,
     query, key, value, taps, weight, first_wide, last_wide, turn, second_wide, first, last, second,
     cot, gated, gated_got, conv, conv_got, grad, grad_got, back, back_got,
     terms_z, terms_y, terms_got_z, terms_got_y, second_z, second_y, second_got_z, second_got_y,
     third_z, third_y, third_got_z, third_got_y, grad_mixed, gate_mixed,
-    grid, mixed, spec, taps_spec, gated_spec, grad_spec, query_res, key_res, value_res, taps_res, weight_res,
-    load_sem, store_sem, gated_sems, conv_sems, grad_sems, back_sems, terms_sems, second_sems, third_sems,
+    grid, mixed, spec, taps_spec, gated_spec, grad_spec,
+    load_sem, gated_sems, conv_sems, grad_sems, back_sems, terms_sems, second_sems, third_sems,
     near_sems, far_sems, relay_sems,
 ):
     terms, terms_got = (terms_z, terms_y), (terms_got_z, terms_got_y)
@@ -197,6 +196,26 @@
 
     key_load = load(0, key_in, key)
     value_load = load(1, value_in, value)
+
+    barrier = pltpu.get_barrier_semaphore()
+
+    def greet(i, carry):
+        pl.semaphore_signal(
+            barrier, inc=1, device_id={"ctx": (me + i) % SEQ_BLOCKS}, device_id_type=pl.DeviceIdType.MESH
+        )
+        return carry
+
+    lax.fori_loop(1, SEQ_BLOCKS, greet, 0)
+    for other in (sibling, across):
+        pl.semaphore_signal(barrier, inc=1, device_id={"tp": other}, device_id_type=pl.DeviceIdType.MESH)
+
+    key_load.wait()
+    value_load.wait()
+
+    def gate(s):
+        gated[s] = (key[s].astype(jnp.float32) * value[s].astype(jnp.float32)).astype(jnp.bfloat16)
+
+    for_blocks(gate)
     cot_load = load(2, cot_in, cot.at[part])
     first_load = load(3, first_in, first_wide)
     turn_load = load(4, turn_in, turn)
@@ -205,26 +224,6 @@
     last_load = load(7, last_in, last_wide)
     weight_load = load(8, weight_in, weight)
     query_load = load(9, query_in, query)
-
-    barrier = pltpu.get_barrier_semaphore()
-
-    def greet(i, carry):
-        pl.semaphore_signal(
-            barrier, inc=1, device_id={"ctx": (me + i) % SEQ_BLOCKS}, device_id_type=pl.DeviceIdType.MESH
-        )
-        return carry
-
-    lax.fori_loop(1, SEQ_BLOCKS, greet, 0)
-    for other in (sibling, across):
-        pl.semaphore_signal(barrier, inc=1, device_id={"tp": other}, device_id_type=pl.DeviceIdType.MESH)
-
-    key_load.wait()
-    value_load.wait()
-
-    def gate(s):
-        gated[s] = (key[s].astype(jnp.float32) * value[s].astype(jnp.float32)).astype(jnp.bfloat16)
-
-    for_blocks(gate)
     pl.semaphore_wait(barrier, SEQ_BLOCKS + 1)
 
     def to_device(source, target, send_sem, recv_sem, device):
@@ -403,11 +402,6 @@
             return (z + k) % 4, {"ctx": (z + k) % 4 * 8 + y * 2 + x}, z
         return (y + k) % 4, {"ctx": z * 8 + (y + k) % 4 * 2 + x}, y
 
-    def chunk_span(order, j):
-        start, stop = TERM_SPANS[order]
-        rows = (stop - start) // TERM_CHUNKS
-        return pl.ds(j * rows, rows)
-
     def first_columns(order, piece):
         if order == 0:
             return pl.ds(0, 1024) if piece == 0 else pl.ds((piece - 1) * 512, 512)
@@ -415,43 +409,42 @@
             return pl.ds(pl.multiple_of(chip * 512, 512), 512)
         return pl.ds(pl.multiple_of((1 - chip) * 512 + (piece - 1) * 256, 256), 256)
 
-    def first_send(order, piece, j, k):
+    def first_send(order, piece, k):
         place, device, own = peer_of(order, 0, k)
-        rows, columns = chunk_span(order, j), first_columns(order, piece)
+        columns = first_columns(order, piece)
         return to_device(
-            terms[order].at[place, rows, columns], terms_got[order].at[own, rows, columns],
-            terms_sems.at[0, order, j, k - 1], terms_sems.at[1, order, j, k - 1], device,
-        )
-
-    def first_whole(order, j, k):
+            terms[order].at[place, :, columns], terms_got[order].at[own, :, columns],
+            terms_sems.at[0, order, piece, k - 1], terms_sems.at[1, order, piece, k - 1], device,
+        )
+
+    def first_arrival(order, piece, k):
         place, device, own = peer_of(order, 0, 4 - k)
-        rows = chunk_span(order, j)
+        columns = first_columns(order, piece)
         return to_device(
-            terms[order].at[place, rows], terms_got[order].at[place, rows],
-            terms_sems.at[0, order, j, k - 1], terms_sems.at[1, order, j, k - 1], device,
-        )
-
-    def second_send(order, j, k):
+            terms[order].at[place, :, columns], terms_got[order].at[place, :, columns],
+            terms_sems.at[0, order, piece, k - 1], terms_sems.at[1, order, piece, k - 1], device,
+        )
+
+    def second_send(order, parity, k):
         place, device, own = peer_of(order, 1, k)
-        rows = chunk_span(order, j)
+        columns = pl.ds(parity * LANES, LANES)
         return to_device(
-            second_terms[order].at[place, rows], second_got[order].at[own, rows],
-            second_sems.at[0, order, j, k - 1], second_sems.at[1, order, j, k - 1], device,
-        )
-
-    def second_arrival(order, j, k):
+            second_terms[order].at[place, :, columns], second_got[order].at[own, :, columns],
+            second_sems.at[0, order, parity, k - 1], second_sems.at[1, order, parity, k - 1], device,
+        )
+
+    def second_arrival(order, parity, k):
         place, device, own = peer_of(order, 1, 4 - k)
-        rows = chunk_span(order, j)
+        columns = pl.ds(parity * LANES, LANES)
         return to_device(
-            second_terms[order].at[place, rows], second_got[order].at[place, rows],
-            second_sems.at[0, order, j, k - 1], second_sems.at[1, order, j, k - 1], device,
-        )
-
-    def side_of(order, j):
-        rows = chunk_span(order, j)
+            second_terms[order].at[place, :, columns], second_got[order].at[place, :, columns],
+            second_sems.at[0, order, parity, k - 1], second_sems.at[1, order, parity, k - 1], device,
+        )
+
+    def side_of(order):
         return to_device(
-            third[order].at[rows], third_got[order].at[rows],
-            third_sems.at[0, order, j], third_sems.at[1, order, j], {"ctx": me + 1 - 2 * x},
+            third[order], third_got[order], third_sems.at[0, order], third_sems.at[1, order],
+            {"ctx": me + 1 - 2 * x},
         )
 
     def keep_term(p, q, parity, term):
@@ -484,15 +477,17 @@
 
         lax.fori_loop(0, 4, step, 0)
 
+    def on_chip(place, piece):
+        here = place // 2 == chip
+        return here if piece == 0 else jnp.logical_not(here)
+
     def send_terms(piece):
-        for j in range(TERM_CHUNKS):
-            for k in (2, 1, 3):
-                first_send(1, piece, j, k).start()
-                here = (z + k) % 4 // 2 == chip
-
-                @pl.when(here if piece == 0 else jnp.logical_not(here))
-                def _():
-                    first_send(0, piece, j, k).start()
+        for k in (2, 1, 3):
+            first_send(1, piece, k).start()
+
+            @pl.when(on_chip((z + k) % 4, piece))
+            def _():
+                first_send(0, piece, k).start()
 
     make_terms()
     send_terms(0)
@@ -511,8 +506,43 @@
         query_res[s] = (grad_mixed[block_rows(s), :] * conv_got[s].astype(jnp.float32)).astype(jnp.bfloat16)
 
     for_blocks(query_gradient)
-    query_store = pltpu.make_async_copy(query_res, query_out, store_sem.at[0])
-    query_store.start()
+
+    def summed(order, stage, held, got, columns):
+        own = z if order == stage else y
+        total = held[order][own, :, columns].astype(jnp.float32)
+        for k in (1, 2, 3):
+            total += got[order][(own + k) % 4, :, columns].astype(jnp.float32)
+        return total
+
+    def first_sum(piece):
+        parities = (0, 1) if piece == 0 else (piece - 1,)
+        owner = chip if piece == 0 else 1 - chip
+        for k in (1, 3, 2):
+            first_arrival(1, piece, k).wait_recv()
+        for parity in parities:
+            for n in range(2):
+                start = pl.multiple_of(owner * 512 + parity * 256 + n * LANES, LANES)
+                total = summed(1, 0, terms, terms_got, pl.ds(start, LANES))
+                second_terms[1][owner * 2 + n, :, pl.ds(parity * LANES, LANES)] = total.astype(jnp.bfloat16)
+        for k in (2, 1, 3):
+
+            @pl.when(on_chip((z + k) % 4, piece))
+            def _():
+                for parity in parities:
+                    second_send(1, parity, k).start()
+
+        @pl.when(on_chip(z, piece))
+        def _():
+            for k in (1, 3, 2):
+                first_arrival(0, piece, k).wait_recv()
+            for parity in parities:
+                for place in range(4):
+                    total = summed(0, 0, terms, terms_got, pl.ds(parity * 512 + place * LANES, LANES))
+                    second_terms[0][place, :, pl.ds(parity * LANES, LANES)] = total.astype(jnp.bfloat16)
+                for k in (2, 1, 3):
+                    second_send(0, parity, k).start()
+
+    first_sum(0)
 
     for half in range(2):
         whole_half(half).wait_recv()
@@ -522,37 +552,13 @@
     signal_of(mixed, last, turn, second, spec, grid)
     give_blocks(grid, back)
     exchange(back, back_got, back_sems)
+    first_sum(1)
     product_to(mixed, gated_spec, grad_spec, True)
     signal_of(mixed, last, turn, second, spec, grid)
     grid_to_taps(grid, taps_res)
-    taps_store = pltpu.make_async_copy(taps_res, taps_out, store_sem.at[1])
-    taps_store.start()
     skip_gradient(grad_got, gated_got, skip_out)
 
-    def summed(order, stage, held, got, j, columns):
-        own = z if order == stage else y
-        rows = chunk_span(order, j)
-        total = held[order][own, rows, columns].astype(jnp.float32)
-        for k in (1, 2, 3):
-            total += got[order][(own + k) % 4, rows, columns].astype(jnp.float32)
-        return total
-
-    for j in range(TERM_CHUNKS):
-        for order in range(2):
-            for k in (1, 3, 2):
-                first_whole(order, j, k).wait_recv()
-            for place in range(4):
-                for parity in range(2):
-                    if order == 0:
-                        start = parity * 512 + place * LANES
-                    else:
-                        start = place // 2 * 512 + parity * 256 + place % 2 * LANES
-                    total = summed(order, 0, terms, terms_got, j, pl.ds(start, LANES))
-                    columns = pl.ds(parity * LANES, LANES)
-                    second_terms[order][place, chunk_span(order, j), columns] = total.astype(jnp.bfloat16)
-            for k in (2, 1, 3):
-                second_send(order, j, k).start()
-
+    first_sum(2)
     arrived(back, back_got, back_sems)
 
     def gate_input(s):
@@ -561,63 +567,58 @@
         value_res[s] = (back_f * key[s].astype(jnp.float32)).astype(jnp.bfloat16)
 
     for_blocks(gate_input)
-    key_store = pltpu.make_async_copy(key_res, key_out, store_sem.at[2])
-    key_store.start()
-    value_store = pltpu.make_async_copy(value_res, value_out, store_sem.at[3])
-    value_store.start()
-    mine = pl.ds(pl.multiple_of(x * LANES, LANES), LANES)
-    others = pl.ds(pl.multiple_of((1 - x) * LANES, LANES), LANES)
-
-    def result_rows(order, j):
-        start, stop = TERM_SPANS[order]
-        rows = (stop - start) // TERM_CHUNKS
-        return pl.ds(start + j * rows, rows)
-
-    for j in range(TERM_CHUNKS):
+    for parity in range(2):
+        columns = pl.ds(parity * LANES, LANES)
         for order in range(2):
             for k in (1, 3, 2):
-                second_arrival(order, j, k).wait_recv()
-            total = summed(order, 1, second_terms, second_got, j, others)
-            third[order][chunk_span(order, j)] = total.astype(jnp.bfloat16)
-            side_of(order, j).start()
-            weight_res[result_rows(order, j), :] = summed(order, 1, second_terms, second_got, j, mine)
-    for j in range(TERM_CHUNKS):
-        for order in range(2):
-            side_of(order, j).wait_recv()
-            weight_res[result_rows(order, j), :] += third_got[order][chunk_span(order, j)].astype(jnp.float32)
-    weight_store = pltpu.make_async_copy(weight_res, weight_out, store_sem.at[4])
-    weight_store.start()
+                second_arrival(order, parity, k).wait_recv()
+
+        @pl.when(x == parity)
+        def _():
+            for order, (start, stop) in enumerate(TERM_SPANS):
+                weight_res[start:stop, :] = summed(order, 1, second_terms, second_got, columns)
+
+        @pl.when(x != parity)
+        def _():
+            for order in range(2):
+                third[order][...] = summed(order, 1, second_terms, second_got, columns).astype(jnp.bfloat16)
+                side_of(order).start()
+
+    for order, (start, stop) in enumerate(TERM_SPANS):
+        side_of(order).wait_recv()
+        weight_res[start:stop, :] += third_got[order][...].astype(jnp.float32)
 
     sent(gated, gated_got, gated_sems)
     sent(conv, conv_got, conv_sems)
     for half in range(2):
         whole_half(half).wait_send()
     sent(back, back_got, back_sems)
-    for j in range(TERM_CHUNKS):
+    for k in (1, 2, 3):
+        for piece in range(3):
+            first_send(1, piece, k).wait_send()
+
+            @pl.when(on_chip((z + k) % 4, piece))
+            def _():
+                first_send(0, piece, k).wait_send()
+
         for order in range(2):
-            for k in (1, 2, 3):
-                first_whole(order, j, k).wait_send()
-                second_send(order, j, k).wait_send()
-            side_of(order, j).wait_send()
+            for parity in range(2):
+                second_send(order, parity, k).wait_send()
+    for order in range(2):
+        side_of(order).wait_send()
     near.wait_send()
     for parity in range(2):
         for half in range(2):
             chunk_bytes(part, parity, half, far_sems, {"tp": across}).wait_send()
             chunk_bytes(across, parity, half, relay_sems, {"tp": sibling}).wait_send()
-    for copy in (query_store, taps_store, key_store, value_store, weight_store):
-        copy.wait()
 
 
 def hand_over(*refs):
-    sources, targets, held, sems = refs[:6], refs[6:12], refs[12:18], refs[18]
-    loads = [pltpu.make_async_copy(a, b, sems.at[0, i]) for i, (a, b) in enumerate(zip(sources, held))]
-    stores = [pltpu.make_async_copy(a, b, sems.at[1, i]) for i, (a, b) in enumerate(zip(held, targets))]
-    for copy in loads:
+    sources, targets, sems = refs[:6], refs[6:12], refs[12]
+    copies = [pltpu.make_async_copy(a, b, sems.at[i]) for i, (a, b) in enumerate(zip(sources, targets))]
+    for copy in copies:
         copy.start()
-    for load, store in zip(loads, stores):
-        load.wait()
-        store.start()
-    for copy in stores:
+    for copy in copies:
         copy.wait()
 
 
@@ -644,9 +645,9 @@
     )
     results = pl.pallas_call(
         kernel,
-        out_shape=shapes,
+        out_shape=tuple(pltpu.VMEM(t.shape, t.dtype) for t in shapes),
         in_specs=[in_hbm] * 4 + [in_vmem] + [in_hbm] * 6,
-        out_specs=[in_hbm] * 4 + [in_vmem, in_hbm],
+        out_specs=[in_vmem] * 6,
         scratch_shapes=[
             block_buffer, block_buffer, block_buffer,
             pltpu.VMEM(filter_taps.shape, f32),
@@ -661,12 +662,9 @@
             pltpu.VMEM((2, CHANS * ROWS, LANES), f32),
             pltpu.VMEM((CHANS * ROWS, 2 * COLS), bf16),
             *[spec_buffer] * 4,
-            block_buffer, block_buffer, block_buffer,
-            pltpu.VMEM(filter_taps.shape, f32),
-            pltpu.VMEM((512, LANES), f32),
-            dma((10,)), dma((5,)),
+            dma((10,)),
             dma((2,)), dma((2,)), dma((2, 2)), dma((2,)),
-            dma((2, 2, TERM_CHUNKS, 3)), dma((2, 2, TERM_CHUNKS, 3)), dma((2, 2, TERM_CHUNKS)),
+            dma((2, 2, 3, 3)), dma((2, 2, 2, 3)), dma((2, 2)),
             dma((2,)), dma((2, 2, 2)), dma((2, 2, 2)),
         ],
         compiler_params=pltpu.CompilerParams(
@@ -679,10 +677,10 @@
     grad_query, grad_key, grad_value, grad_filter, grad_skip, grad_weight = pl.pallas_call(
         hand_over,
         out_shape=shapes,
-        in_specs=[in_hbm] * 6,
+        in_specs=[in_vmem] * 6,
         out_specs=[in_hbm] * 6,
-        scratch_shapes=[*[pltpu.VMEM(t.shape, t.dtype) for t in shapes], dma((2, 6))],
-        compiler_params=pltpu.CompilerParams(vmem_limit_bytes=56 * 1024 * 1024),
+        scratch_shapes=[dma((6,))],
+        compiler_params=pltpu.CompilerParams(vmem_limit_bytes=16 * 1024 * 1024),
     )(*results)
     shape = query_gate.shape
     return (

time: 91.1 us -> 86.6 us (0.951); the launches traced: 90.9 us -> 85.3 us
  Pallas kernels: 90.3 us -> 84.7 us
    pallas_call x2, Pallas kernels: 90.3 us -> 84.7 us  [the longest x1 83.1 us: body(): pl.pallas_call(kernel, out_shape=tuple((pltpu.VMEM(t.shape, t.dtype) for...]
where the time goes in v4:
time: 86.6 us; the launch traced here: 85.3 us
  Pallas kernels  84.7 us (98%)
    pallas_call x1, Pallas kernels, body(): pl.pallas_call(kernel, out_shape=tuple((pltpu.VMEM(t.shape, t.dtype) for...  83.1 us

profile of v4, /device:TPU:1, one launch (start us, length us, event | category | flops | bytes accessed | tf_op | source)
XLA Modules:
  0.0 85.3 jit_solution(16535688819994061027)
XLA Ops:
  0.6 83.1 %shard_map.154 = (bf16[32,16,512]{2,1,0:T(8,128)(2,1)S(1)}, bf16[32,16,512]{2,1,0:T(8,128)(2,1)S(1)}, bf16[32,16,512]{2,1,0:T(8,128)(2,1)S(1)}, f32[16,16384]{1,...) custom-call(bf16[32,16,512]{2,1,0:T(8,128)(2,1)} %bitcast.8, bf16[32,16,512]{2,1,0:T(8,128)(2,1)} %bitcast.9, ...), custom_call_target="tpu_custom_call" | custom-call | tf_op jit(solution)/shard_map/pallas_call | solution.py:646
  83.7 1.6 %shard_map.155 = (bf16[32,16,512]{2,1,0:T(8,128)(2,1)}, bf16[32,16,512]{2,1,0:T(8,128)(2,1)}, bf16[32,16,512]{2,1,0:T(8,128)(2,1)}, f32[16,16384]{1,0:T(8,128)}, f32[1,16]{1,0:T(1,128)}, /*index=5*/f32[512,128]{1,0:T(8,128)}) custom-call(bf16[32,16,512]{2,1,0:T(8,128)(2,1)S(1)} %get-tuple-element.18.refs_0_, ...), custom_call_target="tpu_custom_call" | custom-call | tf_op jit(solution)/shard_map/pallas_call | solution.py:677

commit v5 on v4

--- a/solution.py
+++ b/solution.py
@@ -117,14 +117,10 @@
     lax.fori_loop(0, CHANS, step, 0, unroll=16)
 
 
-def give_blocks(grid, blocks_ref):
-    def step(s, carry):
-        for part in range(4):
-            rows = pl.ds(pl.multiple_of(s * 32 + part // 2 * CHANS, CHANS), CHANS)
-            blocks_ref[s, :, part * LANES : (part + 1) * LANES] = grid[part % 2, rows, :].astype(jnp.bfloat16)
-        return carry
-
-    lax.fori_loop(0, SEQ_BLOCKS, step, 0, unroll=4)
+def give_block(grid, blocks_ref, s):
+    for part in range(4):
+        rows = pl.ds(pl.multiple_of(s * 32 + part // 2 * CHANS, CHANS), CHANS)
+        blocks_ref[s, :, part * LANES : (part + 1) * LANES] = grid[part % 2, rows, :].astype(jnp.bfloat16)
 
 
 def taps_to_grid(taps, skip_ref, grid):
@@ -245,6 +241,20 @@
         lax.fori_loop(1, SEQ_BLOCKS, step, 0)
         target[me] = source[me]
 
+    def give_and_exchange(target_blocks, got, sems):
+        def step(i, carry):
+            peer = (me + i) % SEQ_BLOCKS
+            give_block(grid, target_blocks, peer)
+
+            @pl.when(i < SEQ_BLOCKS)
+            def _():
+                to_device(target_blocks.at[peer], got.at[me], sems.at[0], sems.at[1], {"ctx": peer}).start()
+
+            return carry
+
+        lax.fori_loop(1, SEQ_BLOCKS + 1, step, 0, unroll=4)
+        got[me] = target_blocks[me]
+
     def whole_exchange(source, target, sems):
         blocks = pl.ds(0, SEQ_BLOCKS - 1)
         return to_device(source.at[blocks], target.at[blocks], sems.at[0], sems.at[1], {"tp": across})
@@ -340,8 +350,8 @@
     spectrum_of(grid, first, turn, second, mixed, gated_spec, False)
     product_to(mixed, taps_spec, gated_spec, False)
     signal_of(mixed, last, turn, second, spec, grid)
-    give_blocks(grid, conv)
-    exchange(conv, conv_got, conv_sems)
+    give_and_exchange(conv, conv_got, conv_sems)
+    far_start(0, 1)
 
     def half_exchange(half, source, target, peer):
         columns = pl.ds(half * 256, 256)
@@ -383,7 +393,6 @@
     near.wait_recv()
     mix_features(sibling, False)
     arrived(conv, conv_got, conv_sems)
-    far_start(0, 1)
     far_start(1, 0)
     far_start(1, 1)
 
@@ -550,8 +559,7 @@
     spectrum_of(grid, first, turn, second, mixed, grad_spec, False)
     product_to(mixed, taps_spec, grad_spec, True)
     signal_of(mixed, last, turn, second, spec, grid)
-    give_blocks(grid, back)
-    exchange(back, back_got, back_sems)
+    give_and_exchange(back, back_got, back_sems)
     first_sum(1)
     product_to(mixed, gated_spec, grad_spec, True)
     signal_of(mixed, last, turn, second, spec, grid)

time: 86.6 us -> 85.8 us (level)
  no operation moved by 1% of the time
where the time goes in v5:
time: 85.8 us; the launch traced here: 85.2 us
  Pallas kernels  84.6 us (99%)
    pallas_call x1, Pallas kernels, body(): pl.pallas_call(kernel, out_shape=tuple((pltpu.VMEM(t.shape, t.dtype) for...  82.9 us

profile of v5, /device:TPU:1, one launch (start us, length us, event | category | flops | bytes accessed | tf_op | source)
XLA Modules:
  0.0 85.2 jit_solution(165644237355000452)
XLA Ops:
  0.6 82.9 %shard_map.154 = (bf16[32,16,512]{2,1,0:T(8,128)(2,1)S(1)}, bf16[32,16,512]{2,1,0:T(8,128)(2,1)S(1)}, bf16[32,16,512]{2,1,0:T(8,128)(2,1)S(1)}, f32[16,16384]{1,...) custom-call(bf16[32,16,512]{2,1,0:T(8,128)(2,1)} %bitcast.8, bf16[32,16,512]{2,1,0:T(8,128)(2,1)} %bitcast.9, ...), custom_call_target="tpu_custom_call" | custom-call | tf_op jit(solution)/shard_map/pallas_call | solution.py:654
  83.6 1.6 %shard_map.155 = (bf16[32,16,512]{2,1,0:T(8,128)(2,1)}, bf16[32,16,512]{2,1,0:T(8,128)(2,1)}, bf16[32,16,512]{2,1,0:T(8,128)(2,1)}, f32[16,16384]{1,0:T(8,128)}, f32[1,16]{1,0:T(1,128)}, /*index=5*/f32[512,128]{1,0:T(8,128)}) custom-call(bf16[32,16,512]{2,1,0:T(8,128)(2,1)S(1)} %get-tuple-element.18.refs_0_, ...), custom_call_target="tpu_custom_call" | custom-call | tf_op jit(solution)/shard_map/pallas_call | solution.py:685

commit v6 on v5

--- a/solution.py
+++ b/solution.py
@@ -12,7 +12,7 @@
 LANES = 128
 CHANS = 16
 SEQ_BLOCKS = 32
-Z_FIRST = 192
+Z_FIRST = 208
 TERM_SPANS = ((0, Z_FIRST), (Z_FIRST, 512))
 
 

time: 85.8 us -> 85 us (level); the launches traced: 85.2 us -> 83.6 us
  Pallas kernels: 84.6 us -> 82.9 us
    pallas_call x1, Pallas kernels: 82.9 us -> 81.3 us  [body(): pl.pallas_call(kernel, out_shape=tuple((pltpu.VMEM(t.shape, t.dtype) for...]
where the time goes in v6:
time: 85 us; the launch traced here: 83.6 us
  Pallas kernels  82.9 us (98%)
    pallas_call x1, Pallas kernels, body(): pl.pallas_call(kernel, out_shape=tuple((pltpu.VMEM(t.shape, t.dtype) for...  81.3 us

profile of v6, /device:TPU:1, one launch (start us, length us, event | category | flops | bytes accessed | tf_op | source)
XLA Modules:
  0.0 83.6 jit_solution(13508927473004480388)
XLA Ops:
  0.6 81.3 %shard_map.154 = (bf16[32,16,512]{2,1,0:T(8,128)(2,1)S(1)}, bf16[32,16,512]{2,1,0:T(8,128)(2,1)S(1)}, bf16[32,16,512]{2,1,0:T(8,128)(2,1)S(1)}, f32[16,16384]{1,...) custom-call(bf16[32,16,512]{2,1,0:T(8,128)(2,1)} %bitcast.8, bf16[32,16,512]{2,1,0:T(8,128)(2,1)} %bitcast.9, ...), custom_call_target="tpu_custom_call" | custom-call | tf_op jit(solution)/shard_map/pallas_call | solution.py:654
  81.9 1.6 %shard_map.155 = (bf16[32,16,512]{2,1,0:T(8,128)(2,1)}, bf16[32,16,512]{2,1,0:T(8,128)(2,1)}, bf16[32,16,512]{2,1,0:T(8,128)(2,1)}, f32[16,16384]{1,0:T(8,128)}, f32[1,16]{1,0:T(1,128)}, /*index=5*/f32[512,128]{1,0:T(8,128)}) custom-call(bf16[32,16,512]{2,1,0:T(8,128)(2,1)S(1)} %get-tuple-element.18.refs_0_, ...), custom_call_target="tpu_custom_call" | custom-call | tf_op jit(solution)/shard_map/pallas_call | solution.py:685
